TPU v7x, 512 devices: a whole 4x8x8 slice. The times are simulated.
512 devices in a mesh: bas: 128 (over y, z, core), orb: 4 (over x).
Axes of the slice: x: 4, y: 8, z: 8, core: 2. Of those that a mesh axis runs over, the one named last changes fastest.
Arguments:
- orbitals: bfloat16 [16384, 1024], P('bas', 'orb'), may hold values from -0.046875 to 0.046875
- dipole_orbitals: bfloat16 [3, 16384, 1024], P(None, 'bas', 'orb'), may hold values from -6 to 6
- generator: bfloat16 [1024, 1024], P(None, 'orb'), may hold values from -0.42 to 0.42, as said below
- integrals: bfloat16 [128, 1024, 4096], P('bas', None, 'orb'), may hold values from -6 to 6
Outputs:
- new_orbitals: bfloat16 [16384, 1024], P('bas', 'orb')
- regrouped: bfloat16 [128, 1024, 4096], P(None, 'bas', 'orb')
Inputs may be any that keep to these rules, and one draw needn't show every extreme that they name: generator is antisymmetric: generator[i, j] = -generator[j, i].
All inputs are finite; a program needn't handle non-finite values.
Results may differ from a plain program's by a relative error of at most 0.0049.
Values may be sent and summed in bfloat16 or wider, within the bound.
No kernel may reach another device: no remote copies, remote signals or barrier semaphores. Data moves between devices by JAX's collectives and lax.ppermute only.
A program may use at most 128 MiB of HBM per device.

v0:
```python
import jax
import jax.numpy as jnp
from jax import lax
from jax.sharding import PartitionSpec as P

ORDER = 6


def gradient_of(moments, centers_rows, centers_cols):
    return 4.0 * jnp.sum(moments * (centers_rows[:, :, None] - centers_cols[:, None, :]), axis=0)


def on_device(orbitals, dipole_orbitals, generator, integrals):
    block = orbitals.shape[1]
    nocc = generator.shape[0]
    orb_index = lax.axis_index("orb")
    scale = 1.0 / (16.0 * jnp.sqrt(jnp.float32(nocc)))
    full_orbitals = lax.all_gather(orbitals, "orb", axis=1, tiled=True)
    moments = jnp.einsum(
        "bi,kbj->kij", full_orbitals, dipole_orbitals, preferred_element_type=jnp.float32
    )
    own_rows = lax.dynamic_slice_in_dim(moments, orb_index * block, block, 1)
    centers_part = jnp.diagonal(own_rows, axis1=1, axis2=2)
    summed, centers_own = lax.psum((moments, centers_part), "bas")
    centers_all = lax.all_gather(centers_own, "orb", axis=1, tiled=True)
    gen_cols = gradient_of(summed, centers_all, centers_own) * scale + generator.astype(jnp.float32)
    full_gen = lax.all_gather(gen_cols, "orb", axis=1, tiled=True)
    row_ids = lax.broadcasted_iota(jnp.int32, (nocc, block), 0)
    col_ids = lax.broadcasted_iota(jnp.int32, (nocc, block), 1) + orb_index * block
    term = (row_ids == col_ids).astype(jnp.float32)
    total = term
    for step in range(ORDER):
        term = jnp.dot(full_gen, term, precision=lax.Precision.HIGHEST) / (step + 1.0)
        total = total + term
    rotation = total.astype(jnp.bfloat16)
    new_orbitals = jnp.dot(full_orbitals, rotation, preferred_element_type=jnp.float32).astype(
        jnp.bfloat16
    )
    rotated = jnp.einsum(
        "in,qiv->qnv",
        lax.all_gather(rotation, "orb", axis=1, tiled=True),
        integrals,
        preferred_element_type=jnp.float32,
    ).astype(jnp.bfloat16)
    regrouped = lax.all_to_all(rotated, "bas", split_axis=1, concat_axis=0, tiled=True)
    return (new_orbitals, regrouped)


def solution(mesh):
    return jax.shard_map(
        on_device,
        mesh=mesh,
        in_specs=(P("bas", "orb"), P(None, "bas", "orb"), P(None, "orb"), P("bas", None, "orb")),
        out_specs=(P("bas", "orb"), P(None, "bas", "orb")),
        check_vma=False,
    )
```

profile of v0, /device:TPU:1, one launch (start us, length us, event | category | flops | bytes accessed | tf_op | source)
XLA Modules:
  0.0 809.1 jit_solution(3261129461593968073)
XLA Ops:
  7.2 0.0 copy-start
  7.2 10.9 %all_gather.12 = bf16[128,1024]{1,0:T(8,128)(2,1)S(1)} all-gather(bf16[128,256]{1,0:T(8,128)(2,1)} %param.4), channel_id=1, replica_groups=mesh['bas'=128,'orb'=4] {'orb'}, dimensions={1}, use_global_device_ids=true | all-gather | bytes 327680 | tf_op jit(solution)/shard_map/all_gather | solution.py:18
  18.1 1.5 fusion.9
  19.6 0.0 copy-start.2
  19.6 1.6 copy-done.2
  21.2 0.1 dynamic-slice_bitcast_fusion
  21.3 0.0 all-reduce.2.cloned.1.call-start
  21.4 0.7 all-reduce.2.cloned.1.call-update
  22.0 0.0 all-gather.3.cloned.1.call-start
  22.1 16.8 %copy.24 = f32[3,256,256]{0,2,1:T(8,128)} copy(f32[3,256,256]{1,2,0:T(8,128)S(1)} %dynamic-slice_bitcast_fusion) | data formatting | bytes 1572864 | tf_op jit(solution)/shard_map/dynamic_slice | solution.py:22
  38.9 2.3 gather_fusion
  41.2 498.3 %psum.15 = f32[3,256]{0,1:T(8,128)S(1)} all-reduce(f32[3,256]{0,1:T(8,128)S(1)} %bitcast.48), channel_id=1, replica_groups=mesh['bas'=128,'orb'=4] {'bas'}, use_global_device_ids=true, to_apply=%region_1.2 | all-reduce | flops 768 | bytes 6144 | tf_op jit(solution)/shard_map/psum | solution.py:24
  539.5 0.1 copy.26
  539.6 10.2 %all_gather.13 = f32[3,1024]{0,1:T(8,128)S(1)} all-gather(f32[3,256]{0,1:T(8,128)S(1)} %psum.15), channel_id=1, replica_groups=mesh['bas'=128,'orb'=4] {'orb'}, dimensions={1}, use_global_device_ids=true | all-gather | bytes 15360 | tf_op jit(solution)/shard_map/all_gather | solution.py:25
  549.8 0.2 copy.25
  550.0 1.3 copy.27
  551.2 0.0 all-reduce.2.cloned.1.call-done
  551.3 2.4 multiply_reduce_fusion
  553.7 1.1 convert_add_fusion
  554.8 0.0 all-gather.3.cloned.1.call-update
  554.8 0.2 all-gather.5.cloned.1.call-start
  555.0 53.0 %all-gather.3.cloned.1.call-done = f32[1024,1024]{0,1:T(8,128)} async-done(((f32[1024,256]{0,1:T(8,128)}), f32[1024,1024]{0,1:T(8,128)}) %all-gather.3.cloned.1.call-update) | async-done | bytes 4194320 | tf_op jit(solution)/shard_map/all_gather | solution.py:27
  608.0 0.0 copy-start.1
  608.0 5.8 fusion.7
  613.8 0.0 copy-done.1
  613.8 6.7 convolution_multiply_fusion.4
  620.5 6.9 convolution_multiply_fusion.3
  627.4 6.7 convolution_multiply_fusion.2
  634.2 7.2 convolution_multiply_fusion.1
  641.3 7.8 fusion.5
  649.1 0.0 all-gather.5.cloned.1.call-update
  649.1 39.5 %all-gather.5.cloned.1.call-done = bf16[1024,1024]{1,0:T(8,128)(2,1)} async-done(((bf16[1024,256]{1,0:T(8,128)(2,1)}), bf16[1024,1024]{1,0:T(8,128)(2,1)}) %all-gather.5.cloned.1.call-update) | async-done | bytes 2097168 | tf_op jit(solution)/shard_map/all_gather | solution.py:41
  688.6 0.0 copy-done
  688.6 4.0 convert_bitcast_fusion
  692.6 5.2 copy.35
  697.8 0.5 broadcast.36
  698.3 14.1 %reduce = bf16[1024,1024]{1,0:T(8,128)(2,1)} reduce(bf16[1024,1,1024]{2,1,0:T(2,128)(2,1)} %bitcast.43, bf16[]{:T(256)} %broadcast.36), dimensions={1}, to_apply=%bitcast.42.reduce_sub_computation | reduce | bytes 4194306
  712.4 0.0 copy-start.3
  712.4 4.4 reshape.22
  716.8 15.6 %all-to-all-start = ((bf16[128,2,4096]{2,1,0:T(2,128)(2,1)}), bf16[128,2,4096]{2,1,0:T(2,128)(2,1)}, u32[]{:S(2)}, u32[]{:S(2)}) async-start(bf16[128,2,4096]{2,1,0:T(2,128)(2,1)} %reshape.22), calls=%async_computation | async-start | bytes 4194304 | tf_op jit(solution)/shard_map/all_to_all | solution.py:45
  732.4 0.0 copy-done.3
  732.4 0.3 fusion.6
  732.8 0.7 copy.29
  733.5 50.7 %all-to-all-done = bf16[128,2,4096]{2,1,0:T(2,128)(2,1)} async-done(((bf16[128,2,4096]{2,1,0:T(2,128)(2,1)}), bf16[128,2,4096]{2,1,0:T(2,128)(2,1)}, u32[]{:S(2)}, u32[]{:S(2)}) %all-to-all-start) | async-done | bytes 2097184 | tf_op jit(solution)/shard_map/all_to_all | solution.py:45
  784.2 13.9 %reshape.23 = bf16[1024,1,1024]{2,1,0:T(2,128)(2,1)} reshape(bf16[128,2,4096]{2,1,0:T(2,128)(2,1)} %all-to-all-done) | data formatting | bytes 4194304
  798.1 4.3 copy.34
  (2 shorter events, 0.0 us)
Async XLA Ops:
  7.2 681.4 %copy-start = (bf16[1,1024,1024]{2,1,0:T(8,128)(2,1)S(1)}, bf16[1,1024,1024]{2,1,0:T(8,128)(2,1)}, u32[]{:S(2)}) copy-start(bf16[1,1024,1024]{2,1,0:T(8,128)(2,1)} %param.7) | copy-start | bytes 6291460
  19.6 1.6 copy-start.2
  21.3 530.0 %all-reduce.2.cloned.1.call-start = ((), (), s32[]{:S(2)}) async-start(), calls=%async_computation.1 | async-start | bytes 6291456 | tf_op jit(solution)/shard_map/psum | solution.py:24
  22.0 586.0 %all-gather.3.cloned.1.call-start = ((), (), s32[]{:S(2)}) async-start(), calls=%async_computation.2 | async-start | bytes 5242880 | tf_op jit(solution)/shard_map/all_gather | solution.py:27
  554.8 133.8 %all-gather.5.cloned.1.call-start = ((), (), s32[]{:S(2)}) async-start(), calls=%async_computation.3 | async-start | bytes 2621440 | tf_op jit(solution)/shard_map/all_gather | solution.py:41
  608.0 5.8 copy-start.1
  712.4 20.0 %copy-start.3 = (bf16[1024,256]{1,0:T(8,128)(2,1)S(1)}, bf16[1024,256]{1,0:T(8,128)(2,1)}, u32[]{:S(2)}) copy-start(bf16[1024,256]{1,0:T(8,128)(2,1)} %fusion.5) | copy-start | bytes 1572868
  716.8 67.4 %all-to-all-start = ((bf16[128,2,4096]{2,1,0:T(2,128)(2,1)}), bf16[128,2,4096]{2,1,0:T(2,128)(2,1)}, u32[]{:S(2)}, u32[]{:S(2)}) async-start(bf16[128,2,4096]{2,1,0:T(2,128)(2,1)} %reshape.22), calls=%async_computation | async-start | bytes 4194304 | tf_op jit(solution)/shard_map/all_to_all | solution.py:45
Sparse Core Ops, SparseCore 0:
  25.5 210.1 all-reduce.1
  554.9 53.0 all-gather.2
  649.2 39.3 all-gather.4
where the time goes:
time: 813 us; the launch traced here: 809 us
  blocking collectives  519 us (64%)
  waiting for transfers between devices  144 us (18%)
  local copies, waits for them, and re-layouts  51.3 us (6%)
  matrix products  46.8 us (6%)
  other arithmetic  17.6 us (2%)
  starting transfers between devices  15.9 us (2%)
  between operations  14.1 us (2%)
    psum x1, blocking collectives, on_device(): summed, centers_own = lax.psum((moments, centers_part), 'bas')  498 us
    all_gather x1, waiting for transfers between devices, on_device(): full_gen = lax.all_gather(gen_cols, 'orb', axis=1, tiled=True)  53 us
    all_to_all x1, waiting for transfers between devices, on_device(): lax.all_to_all(rotated, 'bas', split_axis=1, concat_axis=0, tiled=True)  50.7 us
    dot_general x6, matrix products, on_device(): jnp.dot(full_gen, term, precision=lax.Precision.HIGHEST) / (step + 1.0)  41 us
    all_gather x1, waiting for transfers between devices, on_device(): lax.all_gather(rotation, 'orb', axis=1, tiled=True)  39.5 us
    unnamed x14, local copies, waits for them, and re-layouts  26.7 us
    dynamic_slice x2, local copies, waits for them, and re-layouts, on_device(): own_rows = lax.dynamic_slice_in_dim(moments, orb_index * block, block, 1)  16.8 us
  transfers between devices with their start and end apart: 4, of which 3 were waited for; matrix products, arithmetic and copies ran while one was open for 3% of the time, Pallas kernels for 0%

commit v1 on v0

v1 whole, which is shorter than its diff:
```python
import functools

import jax
import jax.numpy as jnp
from jax import lax
from jax.experimental import pallas as pl
from jax.experimental.pallas import tpu as pltpu
from jax.sharding import Mesh, PartitionSpec as P

F32, BF16, F16 = jnp.float32, jnp.bfloat16, jnp.float16
PLANE = ("y", "z")
BAS = ("y", "z", "core")
WIRE_SCALE = 0.0625


def high_low(value):
    high = value.astype(BF16)
    return high, (value - high.astype(F32)).astype(BF16)


def gradient_kernel(scale, c_own, c_other, d_own, d_other, cen_i, cen_j, out):
    contract = (((0,), (0,)), ((), ()))
    for half in range(c_own.shape[0]):
        cols = slice(256 * half, 256 * half + 256)
        total = None
        for k in range(3):
            moment = lax.dot_general(d_own[k], c_own[half], contract, preferred_element_type=F32)
            moment += lax.dot_general(d_other[k], c_other[half], contract, preferred_element_type=F32)
            term = moment * (cen_i[k : k + 1, cols] - cen_j[:, k : k + 1])
            total = term if total is None else total + term
        total = total * scale
        for r in range(16):
            for g in range(2):
                out[4 * r + 2 * half + g] = total[16 * r : 16 * r + 16, 128 * g : 128 * g + 128]


def product(left_h, left_l, right_h, right_l):
    dot = functools.partial(jnp.dot, preferred_element_type=F32)
    return dot(left_h, right_h) + (dot(left_h, right_l) + dot(left_l, right_h))


def series_kernel(
    place, own_h, own_l, other_h, other_l, integrals, orb, rotated, new_orb,
    xh, xl, x2, x2h, x2l, x3h, x3l, qh, ql, rot,
):
    n, tile = 1024, 256
    core, orb_index = place[0], place[1]
    for src_h, src_l, half in ((own_h, own_l, core), (other_h, other_l, 1 - core)):
        for g in range(4):
            cols = pl.ds(pl.multiple_of(half * 512 + 128 * g, 128), 128)
            for xi in range(4):
                for r in range(16):
                    rows = slice(256 * xi + 16 * r, 256 * xi + 16 * r + 16)
                    xh[rows, cols] = src_h[xi, 4 * r + g]
                    xl[rows, cols] = src_l[xi, 4 * r + g]

    def identity(first):
        row = lax.broadcasted_iota(jnp.int32, (n, tile), 0)
        col = lax.broadcasted_iota(jnp.int32, (n, tile), 1) + first
        return (row == col).astype(F32)

    @pl.loop(0, n // tile)
    def _(step):
        cols = pl.ds(pl.multiple_of(step * tile, tile), tile)
        block = product(xh[...], xl[...], xh[:, cols], xl[:, cols])
        x2[:, cols] = block
        x2h[:, cols], x2l[:, cols] = high_low(block)

    @pl.loop(0, n // tile)
    def _(step):
        cols = pl.ds(pl.multiple_of(step * tile, tile), tile)
        block = product(xh[...], xl[...], x2h[:, cols], x2l[:, cols])
        x3h[:, cols], x3l[:, cols] = high_low(block)
        x1 = xh[:, cols].astype(F32) + xl[:, cols].astype(F32)
        rest = identity(step * tile) * (1 / 6) + x1 * (1 / 24) + x2[:, cols] * (1 / 120) + block * (1 / 720)
        qh[:, cols], ql[:, cols] = high_low(rest)

    @pl.loop(0, n // tile)
    def _(step):
        cols = pl.ds(pl.multiple_of(step * tile, tile), tile)
        block = product(x3h[...], x3l[...], qh[:, cols], ql[:, cols])
        x1 = xh[:, cols].astype(F32) + xl[:, cols].astype(F32)
        rot[:, cols] = (block + 0.5 * x2[:, cols] + x1 + identity(step * tile)).astype(BF16)

    @pl.loop(0, n // tile)
    def _(step):
        cols = pl.ds(pl.multiple_of(step * tile, tile), tile)
        rotated[:, cols] = jnp.dot(rot[...], integrals[:, cols], preferred_element_type=F32).astype(BF16)

    own = rot[pl.ds(pl.multiple_of(orb_index * 256, 256), 256), :]
    total = None
    for xi in range(4):
        part = lax.dot_general(
            orb[xi], own[:, 256 * xi : 256 * xi + 256], (((1,), (1,)), ((), ())), preferred_element_type=F32
        )
        total = part if total is None else total + part
    new_orb[...] = total.astype(BF16)


def on_device(orbitals, dipole_orbitals, generator, integrals):
    nbas, block = orbitals.shape
    nocc = generator.shape[0]
    scale = 4.0 / (16.0 * nocc**0.5)
    core, orb_index = lax.axis_index("core"), lax.axis_index("x")
    place = lax.axis_index("y") * 8 + lax.axis_index("z")
    swap = [(0, 1), (1, 0)]

    def spread(value, axes, count):
        copies = jnp.broadcast_to(value[None], (count,) + value.shape)
        return lax.all_to_all(copies, axes, 0, 0, tiled=True)

    d_other = lax.ppermute(dipole_orbitals, "core", swap)

    partial = jnp.sum(orbitals.astype(F32)[None] * dipole_orbitals.astype(F32), axis=1)
    summed = jnp.sum(spread(partial, PLANE, 64), axis=0)
    first = lax.reduce_precision(summed, 8, 7)
    second = lax.reduce_precision(summed - first, 8, 7)
    third = summed - first - second
    parts = jnp.concatenate([first, second, third, jnp.zeros((7, block), F32)], axis=0).astype(BF16)
    met = spread(jnp.concatenate([orbitals, parts], axis=0), ("core", "x"), 8).reshape(2, 4, nbas + 16, block)
    c_own = lax.dynamic_index_in_dim(met, core, 0, keepdims=False)
    c_other = lax.dynamic_index_in_dim(met, 1 - core, 0, keepdims=False)
    cen = met[:, :, nbas : nbas + 9].astype(F32).reshape(2, 4, 3, 3, block)
    cen = cen[:, :, 0] + cen[:, :, 1] + cen[:, :, 2]
    cen = (cen[0] + cen[1]).transpose(1, 0, 2).reshape(3, nocc)
    cen_i = lax.dynamic_slice_in_dim(cen, core * 512, 512, 1)
    cen_j = lax.dynamic_slice_in_dim(cen, orb_index * block, block, 1).T

    pieces = pl.pallas_call(
        functools.partial(gradient_kernel, scale),
        out_shape=jax.ShapeDtypeStruct((64, 16, 128), F32),
        name="gradient",
    )(
        lax.dynamic_slice_in_dim(c_own[:, :nbas], 2 * core, 2, 0),
        lax.dynamic_slice_in_dim(c_other[:, :nbas], 2 * core, 2, 0),
        dipole_orbitals, d_other, cen_i, cen_j,
    )
    given = lax.dynamic_slice(
        generator, (core * 512 + (place % 4) * 128, (place // 4) * 16), (128, 16)
    ).astype(F32).T
    piece = jnp.sum(lax.all_to_all(pieces, PLANE, 0, 0, tiled=True), axis=0) + given
    wire = (piece * WIRE_SCALE).astype(F16)
    half = spread(spread(wire, PLANE, 64), "x", 4)
    other = lax.ppermute(half, "core", swap)

    def pair(value):
        value = value.astype(F32) * (1 / WIRE_SCALE)
        high = lax.reduce_precision(value, 8, 7)
        return high.astype(BF16), (value - high).astype(BF16)

    n = nocc
    vmem = pl.BlockSpec(memory_space=pltpu.VMEM)
    rotated, new_orbitals = pl.pallas_call(
        series_kernel,
        out_shape=(jax.ShapeDtypeStruct((n, n), BF16), jax.ShapeDtypeStruct((nbas, block), BF16)),
        in_specs=[pl.BlockSpec(memory_space=pltpu.SMEM)] + [vmem] * 6,
        out_specs=(vmem, vmem),
        scratch_shapes=[
            pltpu.VMEM((n, n), BF16), pltpu.VMEM((n, n), BF16), pltpu.VMEM((n, n), F32),
            pltpu.VMEM((n, n), BF16), pltpu.VMEM((n, n), BF16), pltpu.VMEM((n, n), BF16),
            pltpu.VMEM((n, n), BF16), pltpu.VMEM((n, n), BF16), pltpu.VMEM((n, n), BF16),
            pltpu.VMEM((n, n), BF16),
        ],
        compiler_params=pltpu.CompilerParams(vmem_limit_bytes=56 << 20),
        name="series",
    )(jnp.stack([core, orb_index]).astype(jnp.int32), *pair(half), *pair(other), integrals[0], c_own[:, :nbas])
    regrouped = lax.all_to_all(rotated.reshape(128, 8, n), BAS, 0, 0, tiled=True)
    return new_orbitals, regrouped


def solution(mesh):
    split = Mesh(mesh.devices.reshape(8, 8, 2, 4), ("y", "z", "core", "x"))
    return jax.shard_map(
        on_device,
        mesh=split,
        in_specs=(P(BAS, "x"), P(None, BAS, "x"), P(None, "x"), P(BAS, None, "x")),
        out_specs=(P(BAS, "x"), P(None, BAS, "x")),
        check_vma=False,
    )
```

time: 813 us -> 217 us (0.27)
  blocking collectives: 519 us -> 122 us
  waiting for transfers between devices: 144 us -> 24.5 us
  matrix products: 46.8 us -> 0 us
  local copies, waits for them, and re-layouts: 51.3 us -> 7.42 us
  Pallas kernels: 0 us -> 34.4 us
  between operations: 14.1 us -> 0.82 us
  other arithmetic: 17.6 us -> 6.27 us
    psum x1 -> x0, blocking collectives: 498 us -> none  [on_device(): summed, centers_own = lax.psum((moments, centers_part), 'bas')]
    all_to_all x0 -> x4, blocking collectives: none -> 122 us  [the longest x3 62.6 us: spread(): return lax.all_to_all(copies, axes, 0, 0, tiled=True)]
    all_gather x2 -> x0, waiting for transfers between devices: 92.5 us -> none  [the longest x1 53 us: on_device(): full_gen = lax.all_gather(gen_cols, 'orb', axis=1, tiled=True)]
    dot_general x9 -> x0, matrix products: 46.8 us -> none  [the longest x6 41 us: on_device(): jnp.dot(full_gen, term, precision=lax.Precision.HIGHEST) / (step + 1.0)]
    pallas_call x0 -> x2, Pallas kernels: none -> 34.4 us  [the longest x1 31.8 us: on_device(): pl.pallas_call(series_kernel, out_shape=(jax.ShapeDtypeStruct((n, n), BF1...]
    all_to_all x1 -> x2, waiting for transfers between devices: 50.7 us -> 24.5 us  [the longest x1 16.4 us: on_device(): lax.all_to_all(pieces, PLANE, 0, 0, tiled=True)]
    unnamed x14 -> x8, local copies, waits for them, and re-layouts: 26.7 us -> 2.06 us
    all_gather x2 -> x0, blocking collectives: 21.1 us -> none  [the longest x1 10.9 us: on_device(): full_orbitals = lax.all_gather(orbitals, 'orb', axis=1, tiled=True)]
  transfers between devices with their start and end apart: 4 -> 4, of which waited for: 3 -> 2; matrix products, arithmetic and copies ran while one was open for 3% -> 3% of each run, Pallas kernels for 0% -> 0%
where the time goes in v1:
time: 217 us; the launch traced here: 216 us
  blocking collectives  122 us (56%)
  Pallas kernels  34.4 us (16%)
  waiting for transfers between devices  24.5 us (11%)
  starting transfers between devices  20.9 us (10%)
  local copies, waits for them, and re-layouts  7.42 us (3%)
  other arithmetic  6.27 us (3%)
    all_to_all x3, blocking collectives, spread(): return lax.all_to_all(copies, axes, 0, 0, tiled=True)  62.6 us
    all_to_all x1, blocking collectives, on_device(): lax.all_to_all(rotated.reshape(128, 8, n), BAS, 0, 0, tiled=True)  59.1 us
    pallas_call x1, Pallas kernels, on_device(): pl.pallas_call(series_kernel, out_shape=(jax.ShapeDtypeStruct((n, n), BF1...  31.8 us
    all_to_all x1, waiting for transfers between devices, on_device(): lax.all_to_all(pieces, PLANE, 0, 0, tiled=True)  16.4 us
    all_to_all x1, waiting for transfers between devices, spread(): return lax.all_to_all(copies, axes, 0, 0, tiled=True)  8.14 us
    all_to_all x1, starting transfers between devices, spread(): return lax.all_to_all(copies, axes, 0, 0, tiled=True)  7.68 us
    ppermute x1, starting transfers between devices, on_device(): other = lax.ppermute(half, 'core', swap)  6.65 us
    all_to_all x1, starting transfers between devices, on_device(): lax.all_to_all(pieces, PLANE, 0, 0, tiled=True)  4.63 us
  transfers between devices with their start and end apart: 4, of which 2 were waited for; matrix products, arithmetic and copies ran while one was open for 3% of the time, Pallas kernels for 0%

profile of v1, /device:TPU:1, one launch (start us, length us, event | category | flops | bytes accessed | tf_op | source)
XLA Modules:
  0.0 216.0 jit_solution(6250666795027539183)
XLA Ops:
  0.6 0.0 copy-start.1
  0.6 0.9 convert_element_type.30
  1.5 1.0 multiply_reduce_fusion
  2.6 29.5 %all_to_all.30 = f32[64,3,256]{2,1,0:T(4,128)S(1)} all-to-all(f32[64,3,256]{2,1,0:T(4,128)S(1)} %broadcast_in_dim.10), channel_id=1, replica_groups=mesh['y'=8,'z'=8,'core'=2,'x'=4] {'y','z'}, dimensions={0} | all-to-all | bytes 393216 | tf_op jit(solution)/shard_map/all_to_all | solution.py:110
  32.1 0.1 reduce_sum.28
  32.2 1.0 concatenate.6
  33.1 0.9 broadcast_in_dim.12
  34.0 7.7 %all-to-all-start.1 = ((bf16[8,144,256]{2,1,0:T(8,128)(2,1)}), bf16[8,144,256]{2,1,0:T(8,128)(2,1)S(1)}, u32[]{:S(2)}, u32[]{:S(2)}) async-start(bf16[8,144,256]{2,1,0:T(8,128)(2,1)} %broadcast_in_dim.12), calls=%async_computation.1 | async-start | bytes 1179648 | tf_op jit(solution)/shard_map/all_to_all | solution.py:110
  41.7 0.0 copy-done.1
  41.7 1.9 collective-permute-start
  43.6 8.1 %all-to-all-done.1 = bf16[8,144,256]{2,1,0:T(8,128)(2,1)S(1)} async-done(((bf16[8,144,256]{2,1,0:T(8,128)(2,1)}), bf16[8,144,256]{2,1,0:T(8,128)(2,1)S(1)}, u32[]{:S(2)}, u32[]{:S(2)}) %all-to-all-start.1) | async-done | bytes 589856 | tf_op jit(solution)/shard_map/all_to_all | solution.py:110
  51.7 0.1 copy.29
  51.9 0.0 copy-start
  52.0 0.2 copy.30
  52.2 0.7 copy.31.cen_i
  52.9 0.7 dynamic-slice_bitcast_fusion.2.cen_j
  53.6 0.7 constant_dynamic-slice_fusion.1
  54.3 0.0 collective-permute-done.d_other
  54.3 0.0 copy-start.2
  54.3 0.7 copy-done.2
  55.0 2.7 %gradient.1 = f32[64,16,128]{2,1,0:T(8,128)} custom-call(bf16[2,128,256]{2,1,0:T(8,128)(2,1)} %get-tuple-element.16.c_own, bf16[2,128,256]{2,1,0:T(8,128)(2,1)} %get-tuple-element.15.c_other, bf16[3,128,256]{2,1,0:T(8,128)(2,1)} %d_own.1, bf16[3,128,256]{2,1,0:T(8,128)(2,1)} %copy-done.2, f32[3,512]{1,0:T(4,128)} %copy.31.cen_i, ...), custom_call_target="tpu_custom_call" | custom-call | tf_op jit(solution)/shard_map/gradient/pallas_call | solution.py:129
  57.6 0.0 copy-done
  57.6 4.6 %all-to-all-start.2 = ((f32[64,16,128]{2,1,0:T(8,128)}), f32[64,16,128]{2,1,0:T(8,128)S(1)}, u32[]{:S(2)}, u32[]{:S(2)}) async-start(f32[64,16,128]{2,1,0:T(8,128)} %gradient.1), calls=%async_computation.2 | async-start | bytes 1048576 | tf_op jit(solution)/shard_map/all_to_all | solution.py:141
  62.3 0.8 dynamic_slice.28
  63.2 0.1 copy.34
  63.2 16.4 %all-to-all-done.2 = f32[64,16,128]{2,1,0:T(8,128)S(1)} async-done(((f32[64,16,128]{2,1,0:T(8,128)}), f32[64,16,128]{2,1,0:T(8,128)S(1)}, u32[]{:S(2)}, u32[]{:S(2)}) %all-to-all-start.2) | async-done | bytes 524320 | tf_op jit(solution)/shard_map/all_to_all | solution.py:141
  79.6 0.1 reduce_sum.29
  79.7 19.4 %all_to_all.31 = f16[64,16,128]{2,1,0:T(8,128)(2,1)S(1)} all-to-all(f16[64,16,128]{2,1,0:T(8,128)(2,1)S(1)} %broadcast_in_dim.13), channel_id=1, replica_groups=mesh['y'=8,'z'=8,'core'=2,'x'=4] {'y','z'}, dimensions={0} | all-to-all | bytes 524288 | tf_op jit(solution)/shard_map/all_to_all | solution.py:110
  99.1 0.1 broadcast_in_dim.14
  99.3 13.7 %all_to_all.32 = f16[4,64,16,128]{3,2,1,0:T(8,128)(2,1)S(1)} all-to-all(f16[4,64,16,128]{3,2,1,0:T(8,128)(2,1)S(1)} %broadcast_in_dim.14), channel_id=1, replica_groups=mesh['y'=8,'z'=8,'core'=2,'x'=4] {'x'}, dimensions={0} | all-to-all | bytes 2097152 | tf_op jit(solution)/shard_map/all_to_all | solution.py:110
  113.0 6.6 %collective-permute-start.1 = (f16[4,64,16,128]{3,2,1,0:T(8,128)(2,1)S(1)}, f16[4,64,16,128]{3,2,1,0:T(8,128)(2,1)S(1)}, u32[]{:S(2)}, u32[]{:S(2)}) collective-permute-start(f16[4,64,16,128]{3,2,1,0:T(8,128)(2,1)S(1)} %all_to_all.32), channel_id=1, source_target_pairs={{0,4},{4,0},{1,5},{5,1},{2,6},{6,2},{3,7},{7,3},{8,12},{12,8},{9,1... | collective-permute-start | bytes 3145736 | tf_op jit(solution)/shard_map/ppermute | solution.py:144
  119.6 0.7 pad_add_fusion.place
  120.3 1.8 fusion
  122.1 0.0 collective-permute-done.1
  122.1 1.8 fusion.1
  123.8 31.8 %series.1 = (bf16[1024,1024]{1,0:T(8,128)(2,1)}, bf16[128,256]{1,0:T(8,128)(2,1)}) custom-call(s32[2]{0:T(128)} %pad_add_fusion.place, bf16[4,64,16,128]{3,2,1,0:T(8,128)(2,1)} %get-tuple-element.9.own_h, bf16[4,64,16,128]{3,2,1,0:T(8,128)(2,1)} %get-tuple-element.8.own_l, bf16[4,64,16,128]{3,2,1,0:T(8,128)(2,1)} %get-tuple-element.7.other_h, ...), custom_call_target="tpu_custom_call" | custom-call | tf_op jit(solution)/shard_map/series/pallas_call | solution.py:153
  155.6 59.1 %all_to_all.33 = bf16[128,8,1024]{2,1,0:T(8,128)(2,1)S(1)} all-to-all(bf16[128,8,1024]{2,1,0:T(8,128)(2,1)} %bitcast.26), channel_id=1, replica_groups=mesh['y'=8,'z'=8,'core'=2,'x'=4] {'y','z','core'}, dimensions={0} | all-to-all | bytes 4194304 | tf_op jit(solution)/shard_map/all_to_all | solution.py:167
  214.7 1.3 copy.36
  (12 shorter events, 0.2 us)
Async XLA Ops:
  0.6 41.0 %copy-start.1 = (bf16[3,128,256]{2,1,0:T(8,128)(2,1)S(1)}, bf16[3,128,256]{2,1,0:T(8,128)(2,1)}, u32[]{:S(2)}) copy-start(bf16[3,128,256]{2,1,0:T(8,128)(2,1)} %d_own.1) | copy-start | bytes 589828
  34.0 17.8 %all-to-all-start.1 = ((bf16[8,144,256]{2,1,0:T(8,128)(2,1)}), bf16[8,144,256]{2,1,0:T(8,128)(2,1)S(1)}, u32[]{:S(2)}, u32[]{:S(2)}) async-start(bf16[8,144,256]{2,1,0:T(8,128)(2,1)} %broadcast_in_dim.12), calls=%async_computation.1 | async-start | bytes 1179648 | tf_op jit(solution)/shard_map/all_to_all | solution.py:110
  41.7 12.7 %collective-permute-start = (bf16[3,128,256]{2,1,0:T(8,128)(2,1)S(1)}, bf16[3,128,256]{2,1,0:T(8,128)(2,1)S(1)}, u32[]{:S(2)}, u32[]{:S(2)}) collective-permute-start(bf16[3,128,256]{2,1,0:T(8,128)(2,1)S(1)} %copy-done.1), channel_id=1, source_target_pairs={{0,4},{4,0},{1,5},{5,1},{2,6},{6,2},{3,7},{7,3},{8,12},{12,8},{9,1... | collective-permute-start | bytes 589832 | tf_op jit(solution)/shard_map/ppermute | solution.py:112
  51.9 5.7 %copy-start = (bf16[4,128,256]{2,1,0:T(8,128)(2,1)}, bf16[4,128,256]{2,1,0:T(8,128)(2,1)S(1)}, u32[]{:S(2)}) copy-start(bf16[4,128,256]{2,1,0:T(8,128)(2,1)S(1)} %slice.35.orb) | copy-start | bytes 786436
  54.3 0.7 copy-start.2
  57.6 22.0 %all-to-all-start.2 = ((f32[64,16,128]{2,1,0:T(8,128)}), f32[64,16,128]{2,1,0:T(8,128)S(1)}, u32[]{:S(2)}, u32[]{:S(2)}) async-start(f32[64,16,128]{2,1,0:T(8,128)} %gradient.1), calls=%async_computation.2 | async-start | bytes 1048576 | tf_op jit(solution)/shard_map/all_to_all | solution.py:141
  113.0 9.1 %collective-permute-start.1 = (f16[4,64,16,128]{3,2,1,0:T(8,128)(2,1)S(1)}, f16[4,64,16,128]{3,2,1,0:T(8,128)(2,1)S(1)}, u32[]{:S(2)}, u32[]{:S(2)}) collective-permute-start(f16[4,64,16,128]{3,2,1,0:T(8,128)(2,1)S(1)} %all_to_all.32), channel_id=1, source_target_pairs={{0,4},{4,0},{1,5},{5,1},{2,6},{6,2},{3,7},{7,3},{8,12},{12,8},{9,1... | collective-permute-start | bytes 3145736 | tf_op jit(solution)/shard_map/ppermute | solution.py:144

commit v2 on v1

v2 whole, which is shorter than its diff:
```python
import functools

import jax
import jax.numpy as jnp
from jax import lax
from jax.experimental import pallas as pl
from jax.experimental.pallas import tpu as pltpu
from jax.sharding import Mesh, PartitionSpec as P

F32, BF16, F16 = jnp.float32, jnp.bfloat16, jnp.float16
PLANE = ("y", "z")
BAS = ("y", "z", "core")
WIRE_SCALE = 0.0625
def grant(mib):
    return pltpu.CompilerParams(vmem_limit_bytes=mib << 20)


VMEM = pl.BlockSpec(memory_space=pltpu.VMEM)
SMEM = pl.BlockSpec(memory_space=pltpu.SMEM)


def high_low(value):
    high = value.astype(BF16)
    return high, (value - high.astype(F32)).astype(BF16)


def diagonal_kernel(orb, dip, out):
    for k in range(3):
        part = jnp.sum(orb[...].astype(F32) * dip[k].astype(F32), axis=0, keepdims=True)
        for half in range(2):
            line = jnp.broadcast_to(part[:, 128 * half : 128 * half + 128], (out.shape[0], 128))
            out[:, 2 * k + half] = line
    out[:, 6:8] = jnp.zeros((out.shape[0], 2, 128), F32)


def pack_kernel(parts, orb, out):
    total = jnp.sum(parts[...], axis=0)
    first = total.astype(BF16)
    rest = total - first.astype(F32)
    second = rest.astype(BF16)
    third = (rest - second.astype(F32)).astype(BF16)
    tail = jnp.concatenate([first, second, third, jnp.zeros((8, 128), BF16)], axis=0)
    for d in range(out.shape[0]):
        out[d, 0, :128] = orb[:, :128]
        out[d, 1, :128] = orb[:, 128:]
        out[d, 0, 128:] = tail
        out[d, 1, 128:] = jnp.zeros((32, 128), BF16)


def gradient_kernel(scale, place, met, d_own, d_other, out):
    core, orb = place[0], place[1]
    contract = (((0,), (0,)), ((), ()))

    def centers(block):
        total = jnp.zeros((8, 128), F32)
        for source in range(2):
            tail = met[4 * source + block, 0, 128:].astype(F32)
            total = total + (tail[0:8] + tail[8:16] + tail[16:24])
        return total

    mine = centers(orb)
    turned = mine.T
    cen_j = [jnp.concatenate([turned[:, 2 * k : 2 * k + 1], turned[:, 2 * k + 1 : 2 * k + 2]], axis=0) for k in range(3)]
    for half in range(2):
        block = 2 * core + half
        cen_i = centers(block)
        for g in range(2):
            total = None
            for k in range(3):
                moment = lax.dot_general(d_own[k], met[4 * core + block, g, :128], contract, preferred_element_type=F32)
                moment += lax.dot_general(
                    d_other[k], met[4 * (1 - core) + block, g, :128], contract, preferred_element_type=F32
                )
                term = moment * (cen_i[2 * k + g : 2 * k + g + 1] - cen_j[k])
                total = term if total is None else total + term
            total = total * scale
            for r in range(16):
                out[4 * r + 2 * half + g] = total[16 * r : 16 * r + 16]


def product(left_h, left_l, right_h, right_l):
    dot = functools.partial(jnp.dot, preferred_element_type=F32)
    return dot(left_h, right_h) + (dot(left_h, right_l) + dot(left_l, right_h))


def series_kernel(place, own_h, own_l, other_h, other_l, rot, xh, xl, x2h, x2l, qh, ql):
    n, tile = 1024, 256
    core = place[0]
    for src_h, src_l, half in ((own_h, own_l, core), (other_h, other_l, 1 - core)):
        for g in range(4):
            cols = pl.ds(pl.multiple_of(half * 512 + 128 * g, 128), 128)
            for xi in range(4):
                for r in range(16):
                    rows = slice(256 * xi + 16 * r, 256 * xi + 16 * r + 16)
                    xh[rows, cols] = src_h[xi, 4 * r + g]
                    xl[rows, cols] = src_l[xi, 4 * r + g]

    def one(first):
        row = lax.broadcasted_iota(jnp.int32, (n, tile), 0)
        col = lax.broadcasted_iota(jnp.int32, (n, tile), 1) + first
        return (row == col).astype(F32)

    def linear(cols):
        return xh[:, cols].astype(F32) + xl[:, cols].astype(F32)

    @pl.loop(0, n // tile)
    def _(step):
        cols = pl.ds(pl.multiple_of(step * tile, tile), tile)
        square = product(xh[...], xl[...], xh[:, cols], xl[:, cols])
        x2h[:, cols], x2l[:, cols] = high_low(square)
        qh[:, cols], ql[:, cols] = high_low(
            one(step * tile) * (1 / 24) + linear(cols) * (1 / 120) + square * (1 / 720)
        )

    @pl.loop(0, 2)
    def _(step):
        first = core * 512 + step * tile
        cols = pl.ds(pl.multiple_of(first, tile), tile)
        inner = product(x2h[...], x2l[...], qh[:, cols], ql[:, cols])
        qh[:, cols], ql[:, cols] = high_low(one(first) * 0.5 + linear(cols) * (1 / 6) + inner)

    @pl.loop(0, 2)
    def _(step):
        first = core * 512 + step * tile
        cols = pl.ds(pl.multiple_of(first, tile), tile)
        outer = product(x2h[...], x2l[...], qh[:, cols], ql[:, cols])
        rot[:, pl.ds(pl.multiple_of(step * tile, tile), tile)] = (one(first) + linear(cols) + outer).astype(BF16)


def rotate_kernel(place, rot_own, rot_other, integrals, out):
    core, tile = place[0], 256
    near = pl.ds(pl.multiple_of(core * 512, 512), 512)
    far = pl.ds(pl.multiple_of(512 - core * 512, 512), 512)

    @pl.loop(0, 1024 // tile)
    def _(step):
        cols = pl.ds(pl.multiple_of(step * tile, tile), tile)
        total = jnp.dot(rot_own[...], integrals[near, cols], preferred_element_type=F32)
        total += jnp.dot(rot_other[...], integrals[far, cols], preferred_element_type=F32)
        out[:, cols] = total.astype(BF16)


def orbitals_kernel(place, rot_own, rot_other, met, out):
    core, orb = place[0], place[1]
    rows = pl.ds(pl.multiple_of(orb * 256, 256), 256)
    total = None
    for rot, half in ((rot_own, core), (rot_other, 1 - core)):
        mine = rot[rows, :]
        for h in range(2):
            for g in range(2):
                first = 256 * h + 128 * g
                part = lax.dot_general(
                    met[4 * core + 2 * half + h, g, :128], mine[:, first : first + 128],
                    (((1,), (1,)), ((), ())), preferred_element_type=F32,
                )
                total = part if total is None else total + part
    out[...] = total.astype(BF16)


def on_device(orbitals, dipole_orbitals, generator, integrals):
    nbas, block = orbitals.shape
    nocc = generator.shape[0]
    scale = 4.0 / (16.0 * nocc**0.5)
    core, orb_index = lax.axis_index("core"), lax.axis_index("x")
    spot = lax.axis_index("y") * 8 + lax.axis_index("z")
    place = jnp.stack([core, orb_index]).astype(jnp.int32)
    swap = [(0, 1), (1, 0)]

    def spread(value, axes, count):
        copies = jnp.broadcast_to(value[None], (count,) + value.shape)
        return lax.all_to_all(copies, axes, 0, 0, tiled=True)

    partial = pl.pallas_call(
        diagonal_kernel, out_shape=jax.ShapeDtypeStruct((64, 8, 128), F32), name="diagonal"
    )(orbitals, dipole_orbitals)
    partial, d_here, given = lax.optimization_barrier((partial, dipole_orbitals, generator))
    centers = lax.all_to_all(partial, PLANE, 0, 0, tiled=True)
    d_other = lax.ppermute(d_here, "core", swap)
    centers, d_other = lax.optimization_barrier((centers, d_other))
    given = lax.dynamic_slice(given, (core * 512 + (spot % 4) * 128, (spot // 4) * 16), (128, 16)).astype(F32).T
    packed = pl.pallas_call(
        pack_kernel, out_shape=jax.ShapeDtypeStruct((8, 2, nbas + 32, 128), BF16), compiler_params=grant(6), name="pack"
    )(centers, orbitals)
    packed, d_here, given = lax.optimization_barrier((packed, d_here, given))
    met = lax.all_to_all(packed, ("core", "x"), 0, 0, tiled=True)
    pieces = pl.pallas_call(
        functools.partial(gradient_kernel, scale),
        out_shape=jax.ShapeDtypeStruct((64, 16, 128), F32),
        in_specs=[SMEM] + [VMEM] * 3,
        compiler_params=grant(8),
        name="gradient",
    )(place, met, d_here, d_other)
    piece = jnp.sum(lax.all_to_all(pieces, PLANE, 0, 0, tiled=True), axis=0) + given
    wire = (piece * WIRE_SCALE).astype(F16)
    half = spread(spread(wire, PLANE, 64), "x", 4)
    other = lax.ppermute(half, "core", swap)

    def pair(value):
        value = value.astype(F32) * (1 / WIRE_SCALE)
        high = lax.reduce_precision(value, 8, 7)
        return high.astype(BF16), (value - high).astype(BF16)

    n = nocc
    rot_own = pl.pallas_call(
        series_kernel,
        out_shape=jax.ShapeDtypeStruct((n, n // 2), BF16),
        in_specs=[SMEM] + [VMEM] * 4,
        scratch_shapes=[pltpu.VMEM((n, n), BF16)] * 6,
        compiler_params=grant(24),
        name="series",
    )(place, *pair(half), *pair(other))
    rot_other = lax.ppermute(rot_own, "core", swap)
    rotated = pl.pallas_call(
        rotate_kernel,
        out_shape=jax.ShapeDtypeStruct((n, n), BF16),
        in_specs=[SMEM] + [VMEM] * 3,
        compiler_params=grant(16),
        name="rotate",
    )(place, rot_own, rot_other, integrals[0])
    regrouped = lax.all_to_all(rotated.reshape(128, 8, n), BAS, 0, 0, tiled=True)
    new_orbitals = pl.pallas_call(
        orbitals_kernel,
        out_shape=jax.ShapeDtypeStruct((nbas, block), BF16),
        in_specs=[SMEM] + [VMEM] * 3,
        compiler_params=grant(8),
        name="new_orbitals",
    )(place, rot_own, rot_other, met)
    return new_orbitals, regrouped


def solution(mesh):
    split = Mesh(mesh.devices.reshape(8, 8, 2, 4), ("y", "z", "core", "x"))
    return jax.shard_map(
        on_device,
        mesh=split,
        in_specs=(P(BAS, "x"), P(None, BAS, "x"), P(None, "x"), P(BAS, None, "x")),
        out_specs=(P(BAS, "x"), P(None, BAS, "x")),
        check_vma=False,
    )
```

time: 217 us -> 207 us (0.954)
  blocking collectives: 122 us -> 54.3 us
  waiting for transfers between devices: 24.5 us -> 73.3 us
  starting transfers between devices: 20.9 us -> 44.4 us
  Pallas kernels: 34.4 us -> 28.2 us
  other arithmetic: 6.27 us -> 0.98 us
  local copies, waits for them, and re-layouts: 7.42 us -> 4.52 us
    all_to_all x2 -> x3, waiting for transfers between devices: 24.5 us -> 69.4 us  [the longest x1 50.3 us: on_device(): lax.all_to_all(rotated.reshape(128, 8, n), BAS, 0, 0, tiled=True)]
    all_to_all x1, blocking collectives: 59.1 us -> 21.1 us  [on_device(): lax.all_to_all(pieces, PLANE, 0, 0, tiled=True)]
    all_to_all x3 -> x2, blocking collectives: 62.6 us -> 33.2 us  [spread(): return lax.all_to_all(copies, axes, 0, 0, tiled=True)]
    all_to_all x2 -> x3, starting transfers between devices: 12.3 us -> 32.5 us  [the longest x1 17.3 us: on_device(): centers = lax.all_to_all(partial, PLANE, 0, 0, tiled=True)]
    pallas_call x1 -> x5, Pallas kernels: 31.8 us -> 26.8 us  [the longest x1 17.8 us: on_device(): pl.pallas_call(series_kernel, out_shape=jax.ShapeDtypeStruct((n, n // 2),...]
    ppermute x1 -> x2, starting transfers between devices: 1.91 us -> 5.3 us  [the longest x1 2.87 us: on_device(): d_other = lax.ppermute(d_here, 'core', swap)]
    convert_element_type x2, other arithmetic: 3.52 us -> 0.82 us  [pair(): return (high.astype(BF16), (value - high).astype(BF16))]
    dynamic_slice x4 -> x0, local copies, waits for them, and re-layouts: 2.31 us -> none  [the longest x1 0.85 us: on_device(): lax.dynamic_slice(generator, (core * 512 + place % 4 * 128, place // 4 *...]
  transfers between devices with their start and end apart: 4 -> 6, of which waited for: 2 -> 5; matrix products, arithmetic and copies ran while one was open for 3% -> 1% of each run, Pallas kernels for 0% -> 1%
where the time goes in v2:
time: 207 us; the launch traced here: 206 us
  waiting for transfers between devices  73.3 us (35%)
  blocking collectives  54.3 us (26%)
  starting transfers between devices  44.4 us (21%)
  Pallas kernels  28.2 us (14%)
  local copies, waits for them, and re-layouts  4.52 us (2%)
    all_to_all x1, waiting for transfers between devices, on_device(): lax.all_to_all(rotated.reshape(128, 8, n), BAS, 0, 0, tiled=True)  50.3 us
    all_to_all x2, blocking collectives, spread(): return lax.all_to_all(copies, axes, 0, 0, tiled=True)  33.2 us
    all_to_all x1, blocking collectives, on_device(): lax.all_to_all(pieces, PLANE, 0, 0, tiled=True)  21.1 us
    pallas_call x1, Pallas kernels, on_device(): pl.pallas_call(series_kernel, out_shape=jax.ShapeDtypeStruct((n, n // 2),...  17.8 us
    all_to_all x1, starting transfers between devices, on_device(): centers = lax.all_to_all(partial, PLANE, 0, 0, tiled=True)  17.3 us
    all_to_all x1, waiting for transfers between devices, on_device(): met = lax.all_to_all(packed, ('core', 'x'), 0, 0, tiled=True)  10.7 us
    all_to_all x1, waiting for transfers between devices, on_device(): centers = lax.all_to_all(partial, PLANE, 0, 0, tiled=True)  8.35 us
    all_to_all x1, starting transfers between devices, on_device(): met = lax.all_to_all(packed, ('core', 'x'), 0, 0, tiled=True)  7.68 us
  transfers between devices with their start and end apart: 6, of which 5 were waited for; matrix products, arithmetic and copies ran while one was open for 1% of the time, Pallas kernels for 1%

profile of v2, /device:TPU:1, one launch (start us, length us, event | category | flops | bytes accessed | tf_op | source)
XLA Modules:
  0.0 206.5 jit_solution(13686227307748637462)
XLA Ops:
  0.6 0.0 copy-start.2
  0.6 1.8 diagonal.1
  2.5 0.0 copy-start.1
  2.5 17.3 %all-to-all-start = ((f32[64,8,128]{2,1,0:T(8,128)}), f32[64,8,128]{2,1,0:T(8,128)S(1)}, u32[]{:S(2)}, u32[]{:S(2)}) async-start(f32[64,8,128]{2,1,0:T(8,128)} %diagonal.1), calls=%async_computation | async-start | bytes 524288 | tf_op jit(solution)/shard_map/all_to_all | solution.py:177
  19.7 2.9 %collective-permute-start = (bf16[3,128,256]{2,1,0:T(8,128)(2,1)}, bf16[3,128,256]{2,1,0:T(8,128)(2,1)S(1)}, u32[]{:S(2)}, u32[]{:S(2)}) collective-permute-start(bf16[3,128,256]{2,1,0:T(8,128)(2,1)} %d_own), channel_id=1, source_target_pairs={{0,4},{4,0},{1,5},{5,1},{2,6},{6,2},{3,7},{7,3},{8,12},{12,8},{9,1... | collective-permute-start | bytes 589832 | tf_op jit(solution)/shard_map/ppermute | solution.py:178
  22.6 1.2 copy.7
  23.9 0.0 collective-permute-done.d_other
  23.9 8.4 %all-to-all-done.parts = f32[64,8,128]{2,1,0:T(8,128)S(1)} async-done(((f32[64,8,128]{2,1,0:T(8,128)}), f32[64,8,128]{2,1,0:T(8,128)S(1)}, u32[]{:S(2)}, u32[]{:S(2)}) %all-to-all-start) | async-done | bytes 262176 | tf_op jit(solution)/shard_map/all_to_all | solution.py:177
  32.3 0.0 copy-done.2
  32.3 1.0 pack.1
  33.3 7.7 %all-to-all-start.1 = ((bf16[8,2,160,128]{3,2,1,0:T(8,128)(2,1)}), bf16[8,2,160,128]{3,2,1,0:T(8,128)(2,1)S(1)}, u32[]{:S(2)}, u32[]{:S(2)}) async-start(bf16[8,2,160,128]{3,2,1,0:T(8,128)(2,1)} %pack.1), calls=%async_computation.1 | async-start | bytes 1310720 | tf_op jit(solution)/shard_map/all_to_all | solution.py:185
  41.0 0.1 pad_add_fusion.place
  41.0 10.7 %all-to-all-done.1.met = bf16[8,2,160,128]{3,2,1,0:T(8,128)(2,1)S(1)} async-done(((bf16[8,2,160,128]{3,2,1,0:T(8,128)(2,1)}), bf16[8,2,160,128]{3,2,1,0:T(8,128)(2,1)S(1)}, u32[]{:S(2)}, u32[]{:S(2)}) %all-to-all-start.1) | async-done | bytes 655392 | tf_op jit(solution)/shard_map/all_to_all | solution.py:185
  51.7 0.0 copy-done.1
  51.7 1.3 gradient.1
  53.1 21.1 %all_to_all.30 = f32[64,16,128]{2,1,0:T(8,128)S(1)} all-to-all(f32[64,16,128]{2,1,0:T(8,128)S(1)} %gradient.1), channel_id=1, replica_groups=mesh['y'=8,'z'=8,'core'=2,'x'=4] {'y','z'}, dimensions={0} | all-to-all | bytes 1048576 | tf_op jit(solution)/shard_map/all_to_all | solution.py:193
  74.2 0.1 reduce_sum.9
  74.3 19.4 %all_to_all.31 = f16[64,16,128]{2,1,0:T(8,128)(2,1)S(1)} all-to-all(f16[64,16,128]{2,1,0:T(8,128)(2,1)S(1)} %broadcast_in_dim.4), channel_id=1, replica_groups=mesh['y'=8,'z'=8,'core'=2,'x'=4] {'y','z'}, dimensions={0} | all-to-all | bytes 524288 | tf_op jit(solution)/shard_map/all_to_all | solution.py:171
  93.8 0.1 broadcast_in_dim.5
  93.9 13.7 %all_to_all.32 = f16[4,64,16,128]{3,2,1,0:T(8,128)(2,1)S(1)} all-to-all(f16[4,64,16,128]{3,2,1,0:T(8,128)(2,1)S(1)} %broadcast_in_dim.5), channel_id=1, replica_groups=mesh['y'=8,'z'=8,'core'=2,'x'=4] {'x'}, dimensions={0} | all-to-all | bytes 2097152 | tf_op jit(solution)/shard_map/all_to_all | solution.py:171
  107.6 6.6 %collective-permute-start.1 = (f16[4,64,16,128]{3,2,1,0:T(8,128)(2,1)S(1)}, f16[4,64,16,128]{3,2,1,0:T(8,128)(2,1)S(1)}, u32[]{:S(2)}, u32[]{:S(2)}) collective-permute-start(f16[4,64,16,128]{3,2,1,0:T(8,128)(2,1)S(1)} %all_to_all.32), channel_id=1, source_target_pairs={{0,4},{4,0},{1,5},{5,1},{2,6},{6,2},{3,7},{7,3},{8,12},{12,8},{9,1... | collective-permute-start | bytes 3145736 | tf_op jit(solution)/shard_map/ppermute | solution.py:196
  114.3 0.4 fusion
  114.7 1.8 collective-permute-done.1
  116.5 0.4 fusion.1
  116.9 0.0 copy-start
  117.0 17.8 %series.1.rot_own = bf16[1024,512]{1,0:T(8,128)(2,1)S(1)} custom-call(s32[2]{0:T(128)S(1)} %pad_add_fusion.place, bf16[4,64,16,128]{3,2,1,0:T(8,128)(2,1)S(1)} %get-tuple-element.21.own_h, bf16[4,64,16,128]{3,2,1,0:T(8,128)(2,1)S(1)} %get-tuple-element.20.own_l, bf16[4,64,16,128]{3,2,1,0:T(8,128)(2,1)S(1)} %get-tuple-element.19.other_h, ...), custom_call_target="tpu_custom_call" | custom-call | tf_op jit(solution)/shard_map/series/pallas_call | solution.py:204
  134.8 2.4 %collective-permute-start.2 = (bf16[1024,512]{1,0:T(8,128)(2,1)S(1)}, bf16[1024,512]{1,0:T(8,128)(2,1)S(1)}, u32[]{:S(2)}, u32[]{:S(2)}) collective-permute-start(bf16[1024,512]{1,0:T(8,128)(2,1)S(1)} %series.1.rot_own), channel_id=1, source_target_pairs={{0,4},{4,0},{1,5},{5,1},{2,6},{6,2},{3,7},{7,3},{8,12},{12,8},{9,1... | collective-permute-start | bytes 3145736 | tf_op jit(solution)/shard_map/ppermute | solution.py:212
  137.2 2.1 %collective-permute-done.2.rot_other = bf16[1024,512]{1,0:T(8,128)(2,1)S(1)} collective-permute-done((bf16[1024,512]{1,0:T(8,128)(2,1)S(1)}, bf16[1024,512]{1,0:T(8,128)(2,1)S(1)}, u32[]{:S(2)}, u32[]{:S(2)}) %collective-permute-start.2) | collective-permute-done | bytes 1048608 | tf_op jit(solution)/shard_map/ppermute | solution.py:212
  139.3 0.0 copy-done
  139.3 4.8 %rotate.1 = bf16[1024,1024]{1,0:T(8,128)(2,1)} custom-call(s32[2]{0:T(128)S(1)} %pad_add_fusion.place, bf16[1024,512]{1,0:T(8,128)(2,1)S(1)} %series.1.rot_own, bf16[1024,512]{1,0:T(8,128)(2,1)S(1)} %collective-permute-done.2.rot_other, bf16[1024,1024]{1,0:T(8,128)(2,1)S(1)} %bitcast.6), custom_call_target="tpu_custom_call" | custom-call | tf_op jit(solution)/shard_map/rotate/pallas_call | solution.py:213
  144.1 7.5 %all-to-all-start.5 = ((bf16[128,8,1024]{2,1,0:T(8,128)(2,1)}), bf16[128,8,1024]{2,1,0:T(8,128)(2,1)}, u32[]{:S(2)}, u32[]{:S(2)}) async-start(bf16[128,8,1024]{2,1,0:T(8,128)(2,1)} %bitcast.4), calls=%async_computation.5 | async-start | bytes 4194304 | tf_op jit(solution)/shard_map/all_to_all | solution.py:220
  151.6 1.5 new_orbitals.1
  153.1 50.3 %all-to-all-done.5 = bf16[128,8,1024]{2,1,0:T(8,128)(2,1)} async-done(((bf16[128,8,1024]{2,1,0:T(8,128)(2,1)}), bf16[128,8,1024]{2,1,0:T(8,128)(2,1)}, u32[]{:S(2)}, u32[]{:S(2)}) %all-to-all-start.5) | async-done | bytes 2097184 | tf_op jit(solution)/shard_map/all_to_all | solution.py:220
  203.4 3.1 %copy.9 = bf16[128,8,1024]{2,1,0:T(8,128)(2,1)} copy(bf16[128,8,1024]{2,1,0:T(8,128)(2,1)} %all-to-all-done.5) | data formatting | bytes 4194304
  (3 shorter events, 0.1 us)
Async XLA Ops:
  0.6 31.7 %copy-start.2 = (bf16[128,256]{1,0:T(8,128)(2,1)S(1)}, bf16[128,256]{1,0:T(8,128)(2,1)}, u32[]{:S(2)}) copy-start(bf16[128,256]{1,0:T(8,128)(2,1)} %orb.3) | copy-start | bytes 196612
  2.5 49.3 %copy-start.1 = (bf16[3,128,256]{2,1,0:T(8,128)(2,1)S(1)}, bf16[3,128,256]{2,1,0:T(8,128)(2,1)}, u32[]{:S(2)}) copy-start(bf16[3,128,256]{2,1,0:T(8,128)(2,1)} %d_own) | copy-start | bytes 589828
  2.5 29.8 %all-to-all-start = ((f32[64,8,128]{2,1,0:T(8,128)}), f32[64,8,128]{2,1,0:T(8,128)S(1)}, u32[]{:S(2)}, u32[]{:S(2)}) async-start(f32[64,8,128]{2,1,0:T(8,128)} %diagonal.1), calls=%async_computation | async-start | bytes 524288 | tf_op jit(solution)/shard_map/all_to_all | solution.py:177
  19.7 4.2 %collective-permute-start = (bf16[3,128,256]{2,1,0:T(8,128)(2,1)}, bf16[3,128,256]{2,1,0:T(8,128)(2,1)S(1)}, u32[]{:S(2)}, u32[]{:S(2)}) collective-permute-start(bf16[3,128,256]{2,1,0:T(8,128)(2,1)} %d_own), channel_id=1, source_target_pairs={{0,4},{4,0},{1,5},{5,1},{2,6},{6,2},{3,7},{7,3},{8,12},{12,8},{9,1... | collective-permute-start | bytes 589832 | tf_op jit(solution)/shard_map/ppermute | solution.py:178
  33.3 18.5 %all-to-all-start.1 = ((bf16[8,2,160,128]{3,2,1,0:T(8,128)(2,1)}), bf16[8,2,160,128]{3,2,1,0:T(8,128)(2,1)S(1)}, u32[]{:S(2)}, u32[]{:S(2)}) async-start(bf16[8,2,160,128]{3,2,1,0:T(8,128)(2,1)} %pack.1), calls=%async_computation.1 | async-start | bytes 1310720 | tf_op jit(solution)/shard_map/all_to_all | solution.py:185
  107.6 8.9 %collective-permute-start.1 = (f16[4,64,16,128]{3,2,1,0:T(8,128)(2,1)S(1)}, f16[4,64,16,128]{3,2,1,0:T(8,128)(2,1)S(1)}, u32[]{:S(2)}, u32[]{:S(2)}) collective-permute-start(f16[4,64,16,128]{3,2,1,0:T(8,128)(2,1)S(1)} %all_to_all.32), channel_id=1, source_target_pairs={{0,4},{4,0},{1,5},{5,1},{2,6},{6,2},{3,7},{7,3},{8,12},{12,8},{9,1... | collective-permute-start | bytes 3145736 | tf_op jit(solution)/shard_map/ppermute | solution.py:196
  116.9 22.4 %copy-start = (bf16[1,1024,1024]{2,1,0:T(8,128)(2,1)S(1)}, bf16[1,1024,1024]{2,1,0:T(8,128)(2,1)}, u32[]{:S(2)}) copy-start(bf16[1,1024,1024]{2,1,0:T(8,128)(2,1)} %param.7) | copy-start | bytes 6291460
  134.8 4.6 %collective-permute-start.2 = (bf16[1024,512]{1,0:T(8,128)(2,1)S(1)}, bf16[1024,512]{1,0:T(8,128)(2,1)S(1)}, u32[]{:S(2)}, u32[]{:S(2)}) collective-permute-start(bf16[1024,512]{1,0:T(8,128)(2,1)S(1)} %series.1.rot_own), channel_id=1, source_target_pairs={{0,4},{4,0},{1,5},{5,1},{2,6},{6,2},{3,7},{7,3},{8,12},{12,8},{9,1... | collective-permute-start | bytes 3145736 | tf_op jit(solution)/shard_map/ppermute | solution.py:212
  144.1 59.3 %all-to-all-start.5 = ((bf16[128,8,1024]{2,1,0:T(8,128)(2,1)}), bf16[128,8,1024]{2,1,0:T(8,128)(2,1)}, u32[]{:S(2)}, u32[]{:S(2)}) async-start(bf16[128,8,1024]{2,1,0:T(8,128)(2,1)} %bitcast.4), calls=%async_computation.5 | async-start | bytes 4194304 | tf_op jit(solution)/shard_map/all_to_all | solution.py:220

commit v3 on v2

--- a/solution.py
+++ b/solution.py
@@ -84,7 +84,7 @@
 
 
 def series_kernel(place, own_h, own_l, other_h, other_l, rot, xh, xl, x2h, x2l, qh, ql):
-    n, tile = 1024, 256
+    n, tile = 1024, 512
     core = place[0]
     for src_h, src_l, half in ((own_h, own_l, core), (other_h, other_l, 1 - core)):
         for g in range(4):
@@ -112,14 +112,14 @@
             one(step * tile) * (1 / 24) + linear(cols) * (1 / 120) + square * (1 / 720)
         )
 
-    @pl.loop(0, 2)
+    @pl.loop(0, 512 // tile)
     def _(step):
         first = core * 512 + step * tile
         cols = pl.ds(pl.multiple_of(first, tile), tile)
         inner = product(x2h[...], x2l[...], qh[:, cols], ql[:, cols])
         qh[:, cols], ql[:, cols] = high_low(one(first) * 0.5 + linear(cols) * (1 / 6) + inner)
 
-    @pl.loop(0, 2)
+    @pl.loop(0, 512 // tile)
     def _(step):
         first = core * 512 + step * tile
         cols = pl.ds(pl.multiple_of(first, tile), tile)
@@ -128,7 +128,7 @@
 
 
 def rotate_kernel(place, rot_own, rot_other, integrals, out):
-    core, tile = place[0], 256
+    core, tile = place[0], 512
     near = pl.ds(pl.multiple_of(core * 512, 512), 512)
     far = pl.ds(pl.multiple_of(512 - core * 512, 512), 512)
 
@@ -206,7 +206,7 @@
         out_shape=jax.ShapeDtypeStruct((n, n // 2), BF16),
         in_specs=[SMEM] + [VMEM] * 4,
         scratch_shapes=[pltpu.VMEM((n, n), BF16)] * 6,
-        compiler_params=grant(24),
+        compiler_params=grant(28),
         name="series",
     )(place, *pair(half), *pair(other))
     rot_other = lax.ppermute(rot_own, "core", swap)
@@ -222,7 +222,7 @@
         orbitals_kernel,
         out_shape=jax.ShapeDtypeStruct((nbas, block), BF16),
         in_specs=[SMEM] + [VMEM] * 3,
-        compiler_params=grant(8),
+        compiler_params=grant(60),
         name="new_orbitals",
     )(place, rot_own, rot_other, met)
     return new_orbitals, regrouped

time: 207 us -> 204 us (0.986)
  no operation moved by 1% of the time
where the time goes in v3:
time: 204 us
  waiting for transfers between devices  72.5 us (36%)
  blocking collectives  54.2 us (27%)
  starting transfers between devices  43.9 us (22%)
  Pallas kernels  28.4 us (14%)
  local copies, waits for them, and re-layouts  2.78 us (1%)
    all_to_all x1, waiting for transfers between devices, on_device(): lax.all_to_all(rotated.reshape(128, 8, n), BAS, 0, 0, tiled=True)  49.5 us
    all_to_all x2, blocking collectives, spread(): return lax.all_to_all(copies, axes, 0, 0, tiled=True)  33.1 us
    all_to_all x1, blocking collectives, on_device(): lax.all_to_all(pieces, PLANE, 0, 0, tiled=True)  21.1 us
    all_to_all x1, starting transfers between devices, on_device(): centers = lax.all_to_all(partial, PLANE, 0, 0, tiled=True)  17.3 us
    pallas_call x1, Pallas kernels, on_device(): pl.pallas_call(series_kernel, out_shape=jax.ShapeDtypeStruct((n, n // 2),...  17.3 us
    all_to_all x1, waiting for transfers between devices, on_device(): met = lax.all_to_all(packed, ('core', 'x'), 0, 0, tiled=True)  10.7 us
    all_to_all x1, waiting for transfers between devices, on_device(): centers = lax.all_to_all(partial, PLANE, 0, 0, tiled=True)  8.35 us
    all_to_all x1, starting transfers between devices, on_device(): met = lax.all_to_all(packed, ('core', 'x'), 0, 0, tiled=True)  7.68 us
  transfers between devices with their start and end apart: 6, of which 5 were waited for; matrix products, arithmetic and copies ran while one was open for 1% of the time, Pallas kernels for 1%

profile of v3, /device:TPU:1, one launch (start us, length us, event | category | flops | bytes accessed | tf_op | source)
XLA Modules:
  0.0 203.7 jit_solution(5945174388108725790)
XLA Ops:
  0.6 0.0 copy-start.5
  0.6 1.8 diagonal.1
  2.5 0.0 copy-start.4
  2.5 17.3 %all-to-all-start = ((f32[64,8,128]{2,1,0:T(8,128)}), f32[64,8,128]{2,1,0:T(8,128)S(1)}, u32[]{:S(2)}, u32[]{:S(2)}) async-start(f32[64,8,128]{2,1,0:T(8,128)} %diagonal.1), calls=%async_computation | async-start | bytes 524288 | tf_op jit(solution)/shard_map/all_to_all | solution.py:177
  19.7 2.9 %collective-permute-start = (bf16[3,128,256]{2,1,0:T(8,128)(2,1)}, bf16[3,128,256]{2,1,0:T(8,128)(2,1)S(1)}, u32[]{:S(2)}, u32[]{:S(2)}) collective-permute-start(bf16[3,128,256]{2,1,0:T(8,128)(2,1)} %d_own), channel_id=1, source_target_pairs={{0,4},{4,0},{1,5},{5,1},{2,6},{6,2},{3,7},{7,3},{8,12},{12,8},{9,1... | collective-permute-start | bytes 589832 | tf_op jit(solution)/shard_map/ppermute | solution.py:178
  22.6 1.2 copy.7
  23.9 0.0 collective-permute-done.d_other
  23.9 8.4 %all-to-all-done.parts = f32[64,8,128]{2,1,0:T(8,128)S(1)} async-done(((f32[64,8,128]{2,1,0:T(8,128)}), f32[64,8,128]{2,1,0:T(8,128)S(1)}, u32[]{:S(2)}, u32[]{:S(2)}) %all-to-all-start) | async-done | bytes 262176 | tf_op jit(solution)/shard_map/all_to_all | solution.py:177
  32.3 0.0 copy-done.5
  32.3 1.0 pack.1
  33.3 7.7 %all-to-all-start.1 = ((bf16[8,2,160,128]{3,2,1,0:T(8,128)(2,1)}), bf16[8,2,160,128]{3,2,1,0:T(8,128)(2,1)S(1)}, u32[]{:S(2)}, u32[]{:S(2)}) async-start(bf16[8,2,160,128]{3,2,1,0:T(8,128)(2,1)} %pack.1), calls=%async_computation.1 | async-start | bytes 1310720 | tf_op jit(solution)/shard_map/all_to_all | solution.py:185
  41.0 0.1 pad_add_fusion.place
  41.0 0.0 copy-start.6
  41.0 10.7 %all-to-all-done.1.met = bf16[8,2,160,128]{3,2,1,0:T(8,128)(2,1)S(1)} async-done(((bf16[8,2,160,128]{3,2,1,0:T(8,128)(2,1)}), bf16[8,2,160,128]{3,2,1,0:T(8,128)(2,1)S(1)}, u32[]{:S(2)}, u32[]{:S(2)}) %all-to-all-start.1) | async-done | bytes 655392 | tf_op jit(solution)/shard_map/all_to_all | solution.py:185
  51.7 0.0 copy-done.4
  51.7 0.0 copy-start.1
  51.7 1.3 gradient.1
  53.1 21.1 %all_to_all.30 = f32[64,16,128]{2,1,0:T(8,128)S(1)} all-to-all(f32[64,16,128]{2,1,0:T(8,128)S(1)} %gradient.1), channel_id=1, replica_groups=mesh['y'=8,'z'=8,'core'=2,'x'=4] {'y','z'}, dimensions={0} | all-to-all | bytes 1048576 | tf_op jit(solution)/shard_map/all_to_all | solution.py:193
  74.2 0.1 reduce_sum.9
  74.3 19.4 %all_to_all.31 = f16[64,16,128]{2,1,0:T(8,128)(2,1)S(1)} all-to-all(f16[64,16,128]{2,1,0:T(8,128)(2,1)S(1)} %broadcast_in_dim.4), channel_id=1, replica_groups=mesh['y'=8,'z'=8,'core'=2,'x'=4] {'y','z'}, dimensions={0} | all-to-all | bytes 524288 | tf_op jit(solution)/shard_map/all_to_all | solution.py:171
  93.7 0.1 broadcast_in_dim.5
  93.9 0.0 copy-done.1
  93.9 13.7 %all_to_all.32 = f16[4,64,16,128]{3,2,1,0:T(8,128)(2,1)S(1)} all-to-all(f16[4,64,16,128]{3,2,1,0:T(8,128)(2,1)S(1)} %broadcast_in_dim.5), channel_id=1, replica_groups=mesh['y'=8,'z'=8,'core'=2,'x'=4] {'x'}, dimensions={0} | all-to-all | bytes 2097152 | tf_op jit(solution)/shard_map/all_to_all | solution.py:171
  107.6 6.8 %collective-permute-start.1 = (f16[4,64,16,128]{3,2,1,0:T(8,128)(2,1)S(1)}, f16[4,64,16,128]{3,2,1,0:T(8,128)(2,1)S(1)}, u32[]{:S(2)}, u32[]{:S(2)}) collective-permute-start(f16[4,64,16,128]{3,2,1,0:T(8,128)(2,1)S(1)} %all_to_all.32), channel_id=1, source_target_pairs={{0,4},{4,0},{1,5},{5,1},{2,6},{6,2},{3,7},{7,3},{8,12},{12,8},{9,1... | collective-permute-start | bytes 3145736 | tf_op jit(solution)/shard_map/ppermute | solution.py:196
  114.4 0.4 fusion
  114.9 1.7 collective-permute-done.1
  116.5 0.4 fusion.1
  116.9 0.0 copy-start.3
  116.9 17.3 %series.1.rot_own = bf16[1024,512]{1,0:T(8,128)(2,1)S(1)} custom-call(s32[2]{0:T(128)S(1)} %pad_add_fusion.place, bf16[4,64,16,128]{3,2,1,0:T(8,128)(2,1)S(1)} %get-tuple-element.21.own_h, bf16[4,64,16,128]{3,2,1,0:T(8,128)(2,1)S(1)} %get-tuple-element.20.own_l, bf16[4,64,16,128]{3,2,1,0:T(8,128)(2,1)S(1)} %get-tuple-element.19.other_h, ...), custom_call_target="tpu_custom_call" | custom-call | tf_op jit(solution)/shard_map/series/pallas_call | solution.py:204
  134.2 0.0 copy-start
  134.2 2.2 %collective-permute-start.2 = (bf16[1024,512]{1,0:T(8,128)(2,1)S(1)}, bf16[1024,512]{1,0:T(8,128)(2,1)S(1)}, u32[]{:S(2)}, u32[]{:S(2)}) collective-permute-start(bf16[1024,512]{1,0:T(8,128)(2,1)S(1)} %series.1.rot_own), channel_id=1, source_target_pairs={{0,4},{4,0},{1,5},{5,1},{2,6},{6,2},{3,7},{7,3},{8,12},{12,8},{9,1... | collective-permute-start | bytes 3145736 | tf_op jit(solution)/shard_map/ppermute | solution.py:212
  136.4 2.3 %collective-permute-done.2.rot_other = bf16[1024,512]{1,0:T(8,128)(2,1)S(1)} collective-permute-done((bf16[1024,512]{1,0:T(8,128)(2,1)S(1)}, bf16[1024,512]{1,0:T(8,128)(2,1)S(1)}, u32[]{:S(2)}, u32[]{:S(2)}) %collective-permute-start.2) | collective-permute-done | bytes 1048608 | tf_op jit(solution)/shard_map/ppermute | solution.py:212
  138.8 0.0 copy-start.2
  138.8 0.0 copy-done.6
  138.8 0.0 copy-done.3
  138.8 4.4 %rotate.1 = bf16[1024,1024]{1,0:T(8,128)(2,1)} custom-call(s32[2]{0:T(128)S(1)} %pad_add_fusion.place, bf16[1024,512]{1,0:T(8,128)(2,1)S(1)} %series.1.rot_own, bf16[1024,512]{1,0:T(8,128)(2,1)S(1)} %collective-permute-done.2.rot_other, bf16[1024,1024]{1,0:T(8,128)(2,1)S(1)} %bitcast.6), custom_call_target="tpu_custom_call" | custom-call | tf_op jit(solution)/shard_map/rotate/pallas_call | solution.py:213
  143.2 0.0 copy-done
  143.2 0.0 copy-done.2
  143.2 7.0 %all-to-all-start.5 = ((bf16[128,8,1024]{2,1,0:T(8,128)(2,1)}), bf16[128,8,1024]{2,1,0:T(8,128)(2,1)S(1)}, u32[]{:S(2)}, u32[]{:S(2)}) async-start(bf16[128,8,1024]{2,1,0:T(8,128)(2,1)} %bitcast.4), calls=%async_computation.5 | async-start | bytes 4194304 | tf_op jit(solution)/shard_map/all_to_all | solution.py:220
  150.2 2.7 %new_orbitals.1 = bf16[128,256]{1,0:T(8,128)(2,1)} custom-call(s32[2]{0:T(128)} %copy-done.6, bf16[1024,512]{1,0:T(8,128)(2,1)} %copy-done, bf16[1024,512]{1,0:T(8,128)(2,1)} %copy-done.2, bf16[8,2,160,128]{3,2,1,0:T(8,128)(2,1)} %copy-done.1), custom_call_target="tpu_custom_call" | custom-call | tf_op jit(solution)/shard_map/new_orbitals/pallas_call | solution.py:221
  152.9 49.5 %all-to-all-done.5 = bf16[128,8,1024]{2,1,0:T(8,128)(2,1)S(1)} async-done(((bf16[128,8,1024]{2,1,0:T(8,128)(2,1)}), bf16[128,8,1024]{2,1,0:T(8,128)(2,1)S(1)}, u32[]{:S(2)}, u32[]{:S(2)}) %all-to-all-start.5) | async-done | bytes 2097184 | tf_op jit(solution)/shard_map/all_to_all | solution.py:220
  202.3 1.3 copy.9
  (3 shorter events, 0.1 us)
Async XLA Ops:
  0.6 31.7 %copy-start.5 = (bf16[128,256]{1,0:T(8,128)(2,1)S(1)}, bf16[128,256]{1,0:T(8,128)(2,1)}, u32[]{:S(2)}) copy-start(bf16[128,256]{1,0:T(8,128)(2,1)} %orb.3) | copy-start | bytes 196612
  2.5 49.3 %copy-start.4 = (bf16[3,128,256]{2,1,0:T(8,128)(2,1)S(1)}, bf16[3,128,256]{2,1,0:T(8,128)(2,1)}, u32[]{:S(2)}) copy-start(bf16[3,128,256]{2,1,0:T(8,128)(2,1)} %d_own) | copy-start | bytes 589828
  2.5 29.8 %all-to-all-start = ((f32[64,8,128]{2,1,0:T(8,128)}), f32[64,8,128]{2,1,0:T(8,128)S(1)}, u32[]{:S(2)}, u32[]{:S(2)}) async-start(f32[64,8,128]{2,1,0:T(8,128)} %diagonal.1), calls=%async_computation | async-start | bytes 524288 | tf_op jit(solution)/shard_map/all_to_all | solution.py:177
  19.7 4.2 %collective-permute-start = (bf16[3,128,256]{2,1,0:T(8,128)(2,1)}, bf16[3,128,256]{2,1,0:T(8,128)(2,1)S(1)}, u32[]{:S(2)}, u32[]{:S(2)}) collective-permute-start(bf16[3,128,256]{2,1,0:T(8,128)(2,1)} %d_own), channel_id=1, source_target_pairs={{0,4},{4,0},{1,5},{5,1},{2,6},{6,2},{3,7},{7,3},{8,12},{12,8},{9,1... | collective-permute-start | bytes 589832 | tf_op jit(solution)/shard_map/ppermute | solution.py:178
  33.3 18.5 %all-to-all-start.1 = ((bf16[8,2,160,128]{3,2,1,0:T(8,128)(2,1)}), bf16[8,2,160,128]{3,2,1,0:T(8,128)(2,1)S(1)}, u32[]{:S(2)}, u32[]{:S(2)}) async-start(bf16[8,2,160,128]{3,2,1,0:T(8,128)(2,1)} %pack.1), calls=%async_computation.1 | async-start | bytes 1310720 | tf_op jit(solution)/shard_map/all_to_all | solution.py:185
  41.0 97.7 %copy-start.6 = (s32[2]{0:T(128)}, s32[2]{0:T(128)S(1)}, u32[]{:S(2)}) copy-start(s32[2]{0:T(128)S(1)} %pad_add_fusion.place) | copy-start | bytes 28
  51.7 42.1 %copy-start.1 = (bf16[8,2,160,128]{3,2,1,0:T(8,128)(2,1)}, bf16[8,2,160,128]{3,2,1,0:T(8,128)(2,1)S(1)}, u32[]{:S(2)}) copy-start(bf16[8,2,160,128]{3,2,1,0:T(8,128)(2,1)S(1)} %all-to-all-done.1.met) | copy-start | bytes 1966084
  107.6 8.9 %collective-permute-start.1 = (f16[4,64,16,128]{3,2,1,0:T(8,128)(2,1)S(1)}, f16[4,64,16,128]{3,2,1,0:T(8,128)(2,1)S(1)}, u32[]{:S(2)}, u32[]{:S(2)}) collective-permute-start(f16[4,64,16,128]{3,2,1,0:T(8,128)(2,1)S(1)} %all_to_all.32), channel_id=1, source_target_pairs={{0,4},{4,0},{1,5},{5,1},{2,6},{6,2},{3,7},{7,3},{8,12},{12,8},{9,1... | collective-permute-start | bytes 3145736 | tf_op jit(solution)/shard_map/ppermute | solution.py:196
  116.9 21.9 %copy-start.3 = (bf16[1,1024,1024]{2,1,0:T(8,128)(2,1)S(1)}, bf16[1,1024,1024]{2,1,0:T(8,128)(2,1)}, u32[]{:S(2)}) copy-start(bf16[1,1024,1024]{2,1,0:T(8,128)(2,1)} %param.7) | copy-start | bytes 6291460
  134.2 8.9 %copy-start = (bf16[1024,512]{1,0:T(8,128)(2,1)}, bf16[1024,512]{1,0:T(8,128)(2,1)S(1)}, u32[]{:S(2)}) copy-start(bf16[1024,512]{1,0:T(8,128)(2,1)S(1)} %series.1.rot_own) | copy-start | bytes 3145732
  134.2 4.6 %collective-permute-start.2 = (bf16[1024,512]{1,0:T(8,128)(2,1)S(1)}, bf16[1024,512]{1,0:T(8,128)(2,1)S(1)}, u32[]{:S(2)}, u32[]{:S(2)}) collective-permute-start(bf16[1024,512]{1,0:T(8,128)(2,1)S(1)} %series.1.rot_own), channel_id=1, source_target_pairs={{0,4},{4,0},{1,5},{5,1},{2,6},{6,2},{3,7},{7,3},{8,12},{12,8},{9,1... | collective-permute-start | bytes 3145736 | tf_op jit(solution)/shard_map/ppermute | solution.py:212
  138.8 4.4 %copy-start.2 = (bf16[1024,512]{1,0:T(8,128)(2,1)}, bf16[1024,512]{1,0:T(8,128)(2,1)S(1)}, u32[]{:S(2)}) copy-start(bf16[1024,512]{1,0:T(8,128)(2,1)S(1)} %collective-permute-done.2.rot_other) | copy-start | bytes 3145732
  143.2 59.2 %all-to-all-start.5 = ((bf16[128,8,1024]{2,1,0:T(8,128)(2,1)}), bf16[128,8,1024]{2,1,0:T(8,128)(2,1)S(1)}, u32[]{:S(2)}, u32[]{:S(2)}) async-start(bf16[128,8,1024]{2,1,0:T(8,128)(2,1)} %bitcast.4), calls=%async_computation.5 | async-start | bytes 4194304 | tf_op jit(solution)/shard_map/all_to_all | solution.py:220

commit v4 on v3

--- a/solution.py
+++ b/solution.py
@@ -47,14 +47,14 @@
         out[d, 1, 128:] = jnp.zeros((32, 128), BF16)
 
 
-def gradient_kernel(scale, place, met, d_own, d_other, out):
+def gradient_kernel(scale, place, met, met_other, d_own, d_other, out):
     core, orb = place[0], place[1]
     contract = (((0,), (0,)), ((), ()))
 
     def centers(block):
         total = jnp.zeros((8, 128), F32)
-        for source in range(2):
-            tail = met[4 * source + block, 0, 128:].astype(F32)
+        for source in (met, met_other):
+            tail = source[block, 0, 128:].astype(F32)
             total = total + (tail[0:8] + tail[8:16] + tail[16:24])
         return total
 
@@ -67,9 +67,9 @@
         for g in range(2):
             total = None
             for k in range(3):
-                moment = lax.dot_general(d_own[k], met[4 * core + block, g, :128], contract, preferred_element_type=F32)
+                moment = lax.dot_general(d_own[k], met[block, g, :128], contract, preferred_element_type=F32)
                 moment += lax.dot_general(
-                    d_other[k], met[4 * (1 - core) + block, g, :128], contract, preferred_element_type=F32
+                    d_other[k], met_other[block, g, :128], contract, preferred_element_type=F32
                 )
                 term = moment * (cen_i[2 * k + g : 2 * k + g + 1] - cen_j[k])
                 total = term if total is None else total + term
@@ -127,17 +127,25 @@
         rot[:, pl.ds(pl.multiple_of(step * tile, tile), tile)] = (one(first) + linear(cols) + outer).astype(BF16)
 
 
-def rotate_kernel(place, rot_own, rot_other, integrals, out):
-    core, tile = place[0], 512
-    near = pl.ds(pl.multiple_of(core * 512, 512), 512)
-    far = pl.ds(pl.multiple_of(512 - core * 512, 512), 512)
+def near_kernel(place, rot_own, integrals, out):
+    tile = 512
+    near = pl.ds(pl.multiple_of(place[0] * 512, 512), 512)
 
     @pl.loop(0, 1024 // tile)
     def _(step):
         cols = pl.ds(pl.multiple_of(step * tile, tile), tile)
-        total = jnp.dot(rot_own[...], integrals[near, cols], preferred_element_type=F32)
-        total += jnp.dot(rot_other[...], integrals[far, cols], preferred_element_type=F32)
-        out[:, cols] = total.astype(BF16)
+        out[:, cols] = jnp.dot(rot_own[...], integrals[near, cols], preferred_element_type=F32)
+
+
+def rotate_kernel(place, near_part, rot_other, integrals, out):
+    tile = 512
+    far = pl.ds(pl.multiple_of(512 - place[0] * 512, 512), 512)
+
+    @pl.loop(0, 1024 // tile)
+    def _(step):
+        cols = pl.ds(pl.multiple_of(step * tile, tile), tile)
+        total = jnp.dot(rot_other[...], integrals[far, cols], preferred_element_type=F32)
+        out[:, cols] = (near_part[:, cols] + total).astype(BF16)
 
 
 def orbitals_kernel(place, rot_own, rot_other, met, out):
@@ -150,7 +158,7 @@
             for g in range(2):
                 first = 256 * h + 128 * g
                 part = lax.dot_general(
-                    met[4 * core + 2 * half + h, g, :128], mine[:, first : first + 128],
+                    met[2 * half + h, g, :128], mine[:, first : first + 128],
                     (((1,), (1,)), ((), ())), preferred_element_type=F32,
                 )
                 total = part if total is None else total + part
@@ -179,17 +187,18 @@
     centers, d_other = lax.optimization_barrier((centers, d_other))
     given = lax.dynamic_slice(given, (core * 512 + (spot % 4) * 128, (spot // 4) * 16), (128, 16)).astype(F32).T
     packed = pl.pallas_call(
-        pack_kernel, out_shape=jax.ShapeDtypeStruct((8, 2, nbas + 32, 128), BF16), compiler_params=grant(6), name="pack"
+        pack_kernel, out_shape=jax.ShapeDtypeStruct((4, 2, nbas + 32, 128), BF16), compiler_params=grant(6), name="pack"
     )(centers, orbitals)
     packed, d_here, given = lax.optimization_barrier((packed, d_here, given))
-    met = lax.all_to_all(packed, ("core", "x"), 0, 0, tiled=True)
+    met = lax.all_to_all(packed, "x", 0, 0, tiled=True)
+    met_other = lax.ppermute(met, "core", swap)
     pieces = pl.pallas_call(
         functools.partial(gradient_kernel, scale),
         out_shape=jax.ShapeDtypeStruct((64, 16, 128), F32),
-        in_specs=[SMEM] + [VMEM] * 3,
+        in_specs=[SMEM] + [VMEM] * 4,
         compiler_params=grant(8),
         name="gradient",
-    )(place, met, d_here, d_other)
+    )(place, met, met_other, d_here, d_other)
     piece = jnp.sum(lax.all_to_all(pieces, PLANE, 0, 0, tiled=True), axis=0) + given
     wire = (piece * WIRE_SCALE).astype(F16)
     half = spread(spread(wire, PLANE, 64), "x", 4)
@@ -210,13 +219,21 @@
         name="series",
     )(place, *pair(half), *pair(other))
     rot_other = lax.ppermute(rot_own, "core", swap)
+    near_part = pl.pallas_call(
+        near_kernel,
+        out_shape=jax.ShapeDtypeStruct((n, n), F32),
+        in_specs=[SMEM] + [VMEM] * 2,
+        compiler_params=grant(16),
+        cost_estimate=pl.CostEstimate(flops=1 << 30, bytes_accessed=7 << 20, transcendentals=0),
+        name="near",
+    )(place, rot_own, integrals[0])
     rotated = pl.pallas_call(
         rotate_kernel,
         out_shape=jax.ShapeDtypeStruct((n, n), BF16),
         in_specs=[SMEM] + [VMEM] * 3,
         compiler_params=grant(16),
         name="rotate",
-    )(place, rot_own, rot_other, integrals[0])
+    )(place, near_part, rot_other, integrals[0])
     regrouped = lax.all_to_all(rotated.reshape(128, 8, n), BAS, 0, 0, tiled=True)
     new_orbitals = pl.pallas_call(
         orbitals_kernel,

time: 204 us -> 201 us (0.985)
  waiting for transfers between devices: 72.5 us -> 61.1 us
  blocking collectives: 54.2 us -> 64 us
    all_to_all x1 -> x0, waiting for transfers between devices: 10.7 us -> none  [on_device(): met = lax.all_to_all(packed, ('core', 'x'), 0, 0, tiled=True)]
    all_to_all x0 -> x1, blocking collectives: none -> 9.69 us  [on_device(): met = lax.all_to_all(packed, 'x', 0, 0, tiled=True)]
    all_to_all x1 -> x0, starting transfers between devices: 7.68 us -> none  [on_device(): met = lax.all_to_all(packed, ('core', 'x'), 0, 0, tiled=True)]
    ppermute x0 -> x1, starting transfers between devices: none -> 6.71 us  [on_device(): met_other = lax.ppermute(met, 'core', swap)]
  transfers between devices with their start and end apart: 6 -> 6, of which waited for: 5 -> 5; matrix products, arithmetic and copies ran while one was open for 1% -> 1% of each run, Pallas kernels for 1% -> 2%
where the time goes in v4:
time: 201 us
  blocking collectives  64 us (32%)
  waiting for transfers between devices  61.1 us (30%)
  starting transfers between devices  42.7 us (21%)
  Pallas kernels  28.4 us (14%)
  local copies, waits for them, and re-layouts  2.78 us (1%)
    all_to_all x1, waiting for transfers between devices, on_device(): lax.all_to_all(rotated.reshape(128, 8, n), BAS, 0, 0, tiled=True)  49.6 us
    all_to_all x2, blocking collectives, spread(): return lax.all_to_all(copies, axes, 0, 0, tiled=True)  33.2 us
    all_to_all x1, blocking collectives, on_device(): lax.all_to_all(pieces, PLANE, 0, 0, tiled=True)  21.1 us
    pallas_call x1, Pallas kernels, on_device(): pl.pallas_call(series_kernel, out_shape=jax.ShapeDtypeStruct((n, n // 2),...  17.3 us
    all_to_all x1, starting transfers between devices, on_device(): centers = lax.all_to_all(partial, PLANE, 0, 0, tiled=True)  17.1 us
    all_to_all x1, blocking collectives, on_device(): met = lax.all_to_all(packed, 'x', 0, 0, tiled=True)  9.69 us
    all_to_all x1, waiting for transfers between devices, on_device(): centers = lax.all_to_all(partial, PLANE, 0, 0, tiled=True)  8.35 us
    all_to_all x1, starting transfers between devices, on_device(): lax.all_to_all(rotated.reshape(128, 8, n), BAS, 0, 0, tiled=True)  7 us
  transfers between devices with their start and end apart: 6, of which 5 were waited for; matrix products, arithmetic and copies ran while one was open for 1% of the time, Pallas kernels for 2%

profile of v4, /device:TPU:1, one launch (start us, length us, event | category | flops | bytes accessed | tf_op | source)
XLA Modules:
  0.0 200.8 jit_solution(874734945096046109)
XLA Ops:
  0.6 0.0 copy-start.4
  0.6 0.0 copy-start.5
  0.7 1.9 diagonal.1
  2.5 17.1 %all-to-all-start = ((f32[64,8,128]{2,1,0:T(8,128)}), f32[64,8,128]{2,1,0:T(8,128)S(1)}, u32[]{:S(2)}, u32[]{:S(2)}) async-start(f32[64,8,128]{2,1,0:T(8,128)} %diagonal.1), calls=%async_computation | async-start | bytes 524288 | tf_op jit(solution)/shard_map/all_to_all | solution.py:185
  19.6 2.9 %collective-permute-start = (bf16[3,128,256]{2,1,0:T(8,128)(2,1)}, bf16[3,128,256]{2,1,0:T(8,128)(2,1)S(1)}, u32[]{:S(2)}, u32[]{:S(2)}) collective-permute-start(bf16[3,128,256]{2,1,0:T(8,128)(2,1)} %d_own), channel_id=1, source_target_pairs={{0,4},{4,0},{1,5},{5,1},{2,6},{6,2},{3,7},{7,3},{8,12},{12,8},{9,1... | collective-permute-start | bytes 589832 | tf_op jit(solution)/shard_map/ppermute | solution.py:186
  22.6 1.2 copy.7
  23.8 0.0 collective-permute-done.d_other
  23.8 8.4 %all-to-all-done.parts = f32[64,8,128]{2,1,0:T(8,128)S(1)} async-done(((f32[64,8,128]{2,1,0:T(8,128)}), f32[64,8,128]{2,1,0:T(8,128)S(1)}, u32[]{:S(2)}, u32[]{:S(2)}) %all-to-all-start) | async-done | bytes 262176 | tf_op jit(solution)/shard_map/all_to_all | solution.py:185
  32.2 0.0 copy-done.5
  32.2 0.1 pack.1
  32.3 9.7 %all_to_all.30.met = bf16[4,2,160,128]{3,2,1,0:T(8,128)(2,1)S(1)} all-to-all(bf16[4,2,160,128]{3,2,1,0:T(8,128)(2,1)S(1)} %pack.1), channel_id=1, replica_groups=mesh['y'=8,'z'=8,'core'=2,'x'=4] {'x'}, dimensions={0} | all-to-all | bytes 655360 | tf_op jit(solution)/shard_map/all_to_all | solution.py:193
  42.0 0.0 copy-start.3
  42.0 6.7 %collective-permute-start.1 = (bf16[4,2,160,128]{3,2,1,0:T(8,128)(2,1)S(1)}, bf16[4,2,160,128]{3,2,1,0:T(8,128)(2,1)S(1)}, u32[]{:S(2)}, u32[]{:S(2)}) collective-permute-start(bf16[4,2,160,128]{3,2,1,0:T(8,128)(2,1)S(1)} %all_to_all.30.met), channel_id=1, source_target_pairs={{0,4},{4,0},{1,5},{5,1},{2,6},{6,2},{3,7},{7,3},{8,12},{12,8},{9,1... | collective-permute-start | bytes 983048 | tf_op jit(solution)/shard_map/ppermute | solution.py:194
  48.7 0.1 pad_add_fusion.place
  48.8 0.0 copy-start.6
  48.8 1.2 collective-permute-done.1.met_other
  50.0 0.0 copy-done.4
  50.0 1.3 gradient.1
  51.3 21.1 %all_to_all.31 = f32[64,16,128]{2,1,0:T(8,128)S(1)} all-to-all(f32[64,16,128]{2,1,0:T(8,128)S(1)} %gradient.1), channel_id=1, replica_groups=mesh['y'=8,'z'=8,'core'=2,'x'=4] {'y','z'}, dimensions={0} | all-to-all | bytes 1048576 | tf_op jit(solution)/shard_map/all_to_all | solution.py:202
  72.4 0.1 reduce_sum.9
  72.5 19.4 %all_to_all.32 = f16[64,16,128]{2,1,0:T(8,128)(2,1)S(1)} all-to-all(f16[64,16,128]{2,1,0:T(8,128)(2,1)S(1)} %broadcast_in_dim.4), channel_id=1, replica_groups=mesh['y'=8,'z'=8,'core'=2,'x'=4] {'y','z'}, dimensions={0} | all-to-all | bytes 524288 | tf_op jit(solution)/shard_map/all_to_all | solution.py:179
  92.0 0.1 broadcast_in_dim.5
  92.1 0.0 copy-done.3
  92.1 13.7 %all_to_all.33 = f16[4,64,16,128]{3,2,1,0:T(8,128)(2,1)S(1)} all-to-all(f16[4,64,16,128]{3,2,1,0:T(8,128)(2,1)S(1)} %broadcast_in_dim.5), channel_id=1, replica_groups=mesh['y'=8,'z'=8,'core'=2,'x'=4] {'x'}, dimensions={0} | all-to-all | bytes 2097152 | tf_op jit(solution)/shard_map/all_to_all | solution.py:179
  105.8 6.8 %collective-permute-start.2 = (f16[4,64,16,128]{3,2,1,0:T(8,128)(2,1)S(1)}, f16[4,64,16,128]{3,2,1,0:T(8,128)(2,1)S(1)}, u32[]{:S(2)}, u32[]{:S(2)}) collective-permute-start(f16[4,64,16,128]{3,2,1,0:T(8,128)(2,1)S(1)} %all_to_all.33), channel_id=1, source_target_pairs={{0,4},{4,0},{1,5},{5,1},{2,6},{6,2},{3,7},{7,3},{8,12},{12,8},{9,1... | collective-permute-start | bytes 3145736 | tf_op jit(solution)/shard_map/ppermute | solution.py:205
  112.7 0.4 fusion
  113.1 1.7 collective-permute-done.2
  114.8 0.4 fusion.1
  115.2 0.0 copy-start.1
  115.2 17.3 %series.1.rot_own = bf16[1024,512]{1,0:T(8,128)(2,1)S(1)} custom-call(s32[2]{0:T(128)S(1)} %pad_add_fusion.place, bf16[4,64,16,128]{3,2,1,0:T(8,128)(2,1)S(1)} %get-tuple-element.21.own_h, bf16[4,64,16,128]{3,2,1,0:T(8,128)(2,1)S(1)} %get-tuple-element.20.own_l, bf16[4,64,16,128]{3,2,1,0:T(8,128)(2,1)S(1)} %get-tuple-element.19.other_h, ...), custom_call_target="tpu_custom_call" | custom-call | tf_op jit(solution)/shard_map/series/pallas_call | solution.py:213
  132.5 0.0 copy-start
  132.5 2.2 %collective-permute-start.3 = (bf16[1024,512]{1,0:T(8,128)(2,1)S(1)}, bf16[1024,512]{1,0:T(8,128)(2,1)S(1)}, u32[]{:S(2)}, u32[]{:S(2)}) collective-permute-start(bf16[1024,512]{1,0:T(8,128)(2,1)S(1)} %series.1.rot_own), channel_id=1, source_target_pairs={{0,4},{4,0},{1,5},{5,1},{2,6},{6,2},{3,7},{7,3},{8,12},{12,8},{9,1... | collective-permute-start | bytes 3145736 | tf_op jit(solution)/shard_map/ppermute | solution.py:221
  134.7 0.0 copy-done.1
  134.7 2.0 near.1.near_part
  136.6 0.0 copy-done
  136.6 0.4 collective-permute-done.3.rot_other
  137.0 0.0 copy-done.6
  137.0 0.0 copy-start.2
  137.0 3.3 %rotate.1 = bf16[1024,1024]{1,0:T(8,128)(2,1)} custom-call(s32[2]{0:T(128)S(1)} %pad_add_fusion.place, f32[1024,1024]{1,0:T(8,128)S(1)} %near.1.near_part, bf16[1024,512]{1,0:T(8,128)(2,1)S(1)} %collective-permute-done.3.rot_other, bf16[1024,1024]{1,0:T(8,128)(2,1)S(1)} %bitcast.7), custom_call_target="tpu_custom_call" | custom-call | tf_op jit(solution)/shard_map/rotate/pallas_call | solution.py:230
  140.3 0.0 copy-done.2
  140.3 7.0 %all-to-all-start.5 = ((bf16[128,8,1024]{2,1,0:T(8,128)(2,1)}), bf16[128,8,1024]{2,1,0:T(8,128)(2,1)S(1)}, u32[]{:S(2)}, u32[]{:S(2)}) async-start(bf16[128,8,1024]{2,1,0:T(8,128)(2,1)} %bitcast.4), calls=%async_computation.5 | async-start | bytes 4194304 | tf_op jit(solution)/shard_map/all_to_all | solution.py:237
  147.3 2.6 %new_orbitals.1 = bf16[128,256]{1,0:T(8,128)(2,1)} custom-call(s32[2]{0:T(128)} %copy-done.6, bf16[1024,512]{1,0:T(8,128)(2,1)} %copy-done, bf16[1024,512]{1,0:T(8,128)(2,1)} %copy-done.2, bf16[4,2,160,128]{3,2,1,0:T(8,128)(2,1)} %copy-done.3), custom_call_target="tpu_custom_call" | custom-call | tf_op jit(solution)/shard_map/new_orbitals/pallas_call | solution.py:238
  149.9 49.6 %all-to-all-done.5 = bf16[128,8,1024]{2,1,0:T(8,128)(2,1)S(1)} async-done(((bf16[128,8,1024]{2,1,0:T(8,128)(2,1)}), bf16[128,8,1024]{2,1,0:T(8,128)(2,1)S(1)}, u32[]{:S(2)}, u32[]{:S(2)}) %all-to-all-start.5) | async-done | bytes 2097184 | tf_op jit(solution)/shard_map/all_to_all | solution.py:237
  199.5 1.3 copy.9
  (3 shorter events, 0.1 us)
Async XLA Ops:
  0.6 49.3 %copy-start.4 = (bf16[3,128,256]{2,1,0:T(8,128)(2,1)S(1)}, bf16[3,128,256]{2,1,0:T(8,128)(2,1)}, u32[]{:S(2)}) copy-start(bf16[3,128,256]{2,1,0:T(8,128)(2,1)} %d_own) | copy-start | bytes 589828
  0.6 31.6 %copy-start.5 = (bf16[128,256]{1,0:T(8,128)(2,1)S(1)}, bf16[128,256]{1,0:T(8,128)(2,1)}, u32[]{:S(2)}) copy-start(bf16[128,256]{1,0:T(8,128)(2,1)} %orb.3) | copy-start | bytes 196612
  2.5 29.7 %all-to-all-start = ((f32[64,8,128]{2,1,0:T(8,128)}), f32[64,8,128]{2,1,0:T(8,128)S(1)}, u32[]{:S(2)}, u32[]{:S(2)}) async-start(f32[64,8,128]{2,1,0:T(8,128)} %diagonal.1), calls=%async_computation | async-start | bytes 524288 | tf_op jit(solution)/shard_map/all_to_all | solution.py:185
  19.6 4.2 %collective-permute-start = (bf16[3,128,256]{2,1,0:T(8,128)(2,1)}, bf16[3,128,256]{2,1,0:T(8,128)(2,1)S(1)}, u32[]{:S(2)}, u32[]{:S(2)}) collective-permute-start(bf16[3,128,256]{2,1,0:T(8,128)(2,1)} %d_own), channel_id=1, source_target_pairs={{0,4},{4,0},{1,5},{5,1},{2,6},{6,2},{3,7},{7,3},{8,12},{12,8},{9,1... | collective-permute-start | bytes 589832 | tf_op jit(solution)/shard_map/ppermute | solution.py:186
  42.0 50.1 %copy-start.3 = (bf16[4,2,160,128]{3,2,1,0:T(8,128)(2,1)}, bf16[4,2,160,128]{3,2,1,0:T(8,128)(2,1)S(1)}, u32[]{:S(2)}) copy-start(bf16[4,2,160,128]{3,2,1,0:T(8,128)(2,1)S(1)} %all_to_all.30.met) | copy-start | bytes 983044
  42.0 8.0 %collective-permute-start.1 = (bf16[4,2,160,128]{3,2,1,0:T(8,128)(2,1)S(1)}, bf16[4,2,160,128]{3,2,1,0:T(8,128)(2,1)S(1)}, u32[]{:S(2)}, u32[]{:S(2)}) collective-permute-start(bf16[4,2,160,128]{3,2,1,0:T(8,128)(2,1)S(1)} %all_to_all.30.met), channel_id=1, source_target_pairs={{0,4},{4,0},{1,5},{5,1},{2,6},{6,2},{3,7},{7,3},{8,12},{12,8},{9,1... | collective-permute-start | bytes 983048 | tf_op jit(solution)/shard_map/ppermute | solution.py:194
  48.8 88.2 %copy-start.6 = (s32[2]{0:T(128)}, s32[2]{0:T(128)S(1)}, u32[]{:S(2)}) copy-start(s32[2]{0:T(128)S(1)} %pad_add_fusion.place) | copy-start | bytes 28
  105.8 8.9 %collective-permute-start.2 = (f16[4,64,16,128]{3,2,1,0:T(8,128)(2,1)S(1)}, f16[4,64,16,128]{3,2,1,0:T(8,128)(2,1)S(1)}, u32[]{:S(2)}, u32[]{:S(2)}) collective-permute-start(f16[4,64,16,128]{3,2,1,0:T(8,128)(2,1)S(1)} %all_to_all.33), channel_id=1, source_target_pairs={{0,4},{4,0},{1,5},{5,1},{2,6},{6,2},{3,7},{7,3},{8,12},{12,8},{9,1... | collective-permute-start | bytes 3145736 | tf_op jit(solution)/shard_map/ppermute | solution.py:205
  115.2 19.5 %copy-start.1 = (bf16[1,1024,1024]{2,1,0:T(8,128)(2,1)S(1)}, bf16[1,1024,1024]{2,1,0:T(8,128)(2,1)}, u32[]{:S(2)}) copy-start(bf16[1,1024,1024]{2,1,0:T(8,128)(2,1)} %param.7) | copy-start | bytes 6291460
  132.5 4.2 %copy-start = (bf16[1024,512]{1,0:T(8,128)(2,1)}, bf16[1024,512]{1,0:T(8,128)(2,1)S(1)}, u32[]{:S(2)}) copy-start(bf16[1024,512]{1,0:T(8,128)(2,1)S(1)} %series.1.rot_own) | copy-start | bytes 3145732
  132.5 4.6 %collective-permute-start.3 = (bf16[1024,512]{1,0:T(8,128)(2,1)S(1)}, bf16[1024,512]{1,0:T(8,128)(2,1)S(1)}, u32[]{:S(2)}, u32[]{:S(2)}) collective-permute-start(bf16[1024,512]{1,0:T(8,128)(2,1)S(1)} %series.1.rot_own), channel_id=1, source_target_pairs={{0,4},{4,0},{1,5},{5,1},{2,6},{6,2},{3,7},{7,3},{8,12},{12,8},{9,1... | collective-permute-start | bytes 3145736 | tf_op jit(solution)/shard_map/ppermute | solution.py:221
  137.0 3.3 %copy-start.2 = (bf16[1024,512]{1,0:T(8,128)(2,1)}, bf16[1024,512]{1,0:T(8,128)(2,1)S(1)}, u32[]{:S(2)}) copy-start(bf16[1024,512]{1,0:T(8,128)(2,1)S(1)} %collective-permute-done.3.rot_other) | copy-start | bytes 3145732
  140.3 59.2 %all-to-all-start.5 = ((bf16[128,8,1024]{2,1,0:T(8,128)(2,1)}), bf16[128,8,1024]{2,1,0:T(8,128)(2,1)S(1)}, u32[]{:S(2)}, u32[]{:S(2)}) async-start(bf16[128,8,1024]{2,1,0:T(8,128)(2,1)} %bitcast.4), calls=%async_computation.5 | async-start | bytes 4194304 | tf_op jit(solution)/shard_map/all_to_all | solution.py:237

commit v5 on v4

--- a/solution.py
+++ b/solution.py
@@ -83,48 +83,47 @@
     return dot(left_h, right_h) + (dot(left_h, right_l) + dot(left_l, right_h))
 
 
-def series_kernel(place, own_h, own_l, other_h, other_l, rot, xh, xl, x2h, x2l, qh, ql):
+def assemble(half, src_h, src_l, high, low):
+    for g in range(4):
+        cols = pl.ds(pl.multiple_of(half * 512 + 128 * g, 128), 128)
+        for xi in range(4):
+            for r in range(16):
+                rows = slice(256 * xi + 16 * r, 256 * xi + 16 * r + 16)
+                high[rows, cols] = src_h[xi, 4 * r + g]
+                low[rows, cols] = src_l[xi, 4 * r + g]
+
+
+def square_kernel(place, own_h, own_l, out, high, low):
+    assemble(0, own_h, own_l, high, low)
+    rows = pl.ds(pl.multiple_of(place[0] * 512, 512), 512)
+    out[...] = product(high[...], low[...], high[rows, :], low[rows, :])
+
+
+def series_kernel(place, near_square, own_h, own_l, other_h, other_l, rot, xh, xl, x2h, x2l, qh, ql):
     n, tile = 1024, 512
     core = place[0]
-    for src_h, src_l, half in ((own_h, own_l, core), (other_h, other_l, 1 - core)):
-        for g in range(4):
-            cols = pl.ds(pl.multiple_of(half * 512 + 128 * g, 128), 128)
-            for xi in range(4):
-                for r in range(16):
-                    rows = slice(256 * xi + 16 * r, 256 * xi + 16 * r + 16)
-                    xh[rows, cols] = src_h[xi, 4 * r + g]
-                    xl[rows, cols] = src_l[xi, 4 * r + g]
-
-    def one(first):
+    assemble(core, own_h, own_l, xh, xl)
+    assemble(1 - core, other_h, other_l, xh, xl)
+    first = core * tile
+    near = pl.ds(pl.multiple_of(first, tile), tile)
+    far = pl.ds(pl.multiple_of(tile - first, tile), tile)
+
+    def one():
         row = lax.broadcasted_iota(jnp.int32, (n, tile), 0)
         col = lax.broadcasted_iota(jnp.int32, (n, tile), 1) + first
         return (row == col).astype(F32)
 
-    def linear(cols):
-        return xh[:, cols].astype(F32) + xl[:, cols].astype(F32)
-
-    @pl.loop(0, n // tile)
-    def _(step):
-        cols = pl.ds(pl.multiple_of(step * tile, tile), tile)
-        square = product(xh[...], xl[...], xh[:, cols], xl[:, cols])
-        x2h[:, cols], x2l[:, cols] = high_low(square)
-        qh[:, cols], ql[:, cols] = high_low(
-            one(step * tile) * (1 / 24) + linear(cols) * (1 / 120) + square * (1 / 720)
-        )
-
-    @pl.loop(0, 512 // tile)
-    def _(step):
-        first = core * 512 + step * tile
-        cols = pl.ds(pl.multiple_of(first, tile), tile)
-        inner = product(x2h[...], x2l[...], qh[:, cols], ql[:, cols])
-        qh[:, cols], ql[:, cols] = high_low(one(first) * 0.5 + linear(cols) * (1 / 6) + inner)
-
-    @pl.loop(0, 512 // tile)
-    def _(step):
-        first = core * 512 + step * tile
-        cols = pl.ds(pl.multiple_of(first, tile), tile)
-        outer = product(x2h[...], x2l[...], qh[:, cols], ql[:, cols])
-        rot[:, pl.ds(pl.multiple_of(step * tile, tile), tile)] = (one(first) + linear(cols) + outer).astype(BF16)
+    def linear():
+        return xh[:, near].astype(F32) + xl[:, near].astype(F32)
+
+    square = near_square[...] + product(xh[:, far], xl[:, far], xh[far, near], xl[far, near])
+    x2h[:, near], x2l[:, near] = high_low(square)
+    qh[...], ql[...] = high_low(one() * (1 / 24) + linear() * (1 / 120) + square * (1 / 720))
+    x2h[:, far], x2l[:, far] = high_low(product(xh[...], xl[...], xh[:, far], xl[:, far]))
+    inner = product(x2h[...], x2l[...], qh[...], ql[...])
+    qh[...], ql[...] = high_low(one() * 0.5 + linear() * (1 / 6) + inner)
+    outer = product(x2h[...], x2l[...], qh[...], ql[...])
+    rot[...] = (one() + linear() + outer).astype(BF16)
 
 
 def near_kernel(place, rot_own, integrals, out):
@@ -210,14 +209,24 @@
         return high.astype(BF16), (value - high).astype(BF16)
 
     n = nocc
+    own_pair = pair(half)
+    near_square = pl.pallas_call(
+        square_kernel,
+        out_shape=jax.ShapeDtypeStruct((n, n // 2), F32),
+        in_specs=[SMEM] + [VMEM] * 2,
+        scratch_shapes=[pltpu.VMEM((n, n // 2), BF16)] * 2,
+        compiler_params=grant(12),
+        cost_estimate=pl.CostEstimate(flops=3 << 29, bytes_accessed=4 << 20, transcendentals=0),
+        name="square",
+    )(place, *own_pair)
     rot_own = pl.pallas_call(
         series_kernel,
         out_shape=jax.ShapeDtypeStruct((n, n // 2), BF16),
-        in_specs=[SMEM] + [VMEM] * 4,
-        scratch_shapes=[pltpu.VMEM((n, n), BF16)] * 6,
+        in_specs=[SMEM] + [VMEM] * 5,
+        scratch_shapes=[pltpu.VMEM((n, n), BF16)] * 4 + [pltpu.VMEM((n, n // 2), BF16)] * 2,
         compiler_params=grant(28),
         name="series",
-    )(place, *pair(half), *pair(other))
+    )(place, near_square, *own_pair, *pair(other))
     rot_other = lax.ppermute(rot_own, "core", swap)
     near_part = pl.pallas_call(
         near_kernel,

time: 201 us -> 199 us (0.990)
    pallas_call x1, Pallas kernels: 17.3 us -> 14 us  [on_device(): pl.pallas_call(series_kernel, out_shape=jax.ShapeDtypeStruct((n, n // 2),...]
    pallas_call x0 -> x1, Pallas kernels: none -> 2.53 us  [on_device(): pl.pallas_call(square_kernel, out_shape=jax.ShapeDtypeStruct((n, n // 2),...]
  transfers between devices with their start and end apart: 6 -> 6, of which waited for: 5 -> 4; matrix products, arithmetic and copies ran while one was open for 1% -> 1% of each run, Pallas kernels for 2% -> 4%
where the time goes in v5:
time: 199 us; the launch traced here: 198 us
  blocking collectives  64 us (32%)
  waiting for transfers between devices  59.7 us (30%)
  starting transfers between devices  42.3 us (21%)
  Pallas kernels  27.6 us (14%)
  local copies, waits for them, and re-layouts  2.78 us (1%)
    all_to_all x1, waiting for transfers between devices, on_device(): lax.all_to_all(rotated.reshape(128, 8, n), BAS, 0, 0, tiled=True)  49.6 us
    all_to_all x2, blocking collectives, spread(): return lax.all_to_all(copies, axes, 0, 0, tiled=True)  33.2 us
    all_to_all x1, blocking collectives, on_device(): lax.all_to_all(pieces, PLANE, 0, 0, tiled=True)  21.1 us
    all_to_all x1, starting transfers between devices, on_device(): centers = lax.all_to_all(partial, PLANE, 0, 0, tiled=True)  17.1 us
    pallas_call x1, Pallas kernels, on_device(): pl.pallas_call(series_kernel, out_shape=jax.ShapeDtypeStruct((n, n // 2),...  14 us
    all_to_all x1, blocking collectives, on_device(): met = lax.all_to_all(packed, 'x', 0, 0, tiled=True)  9.69 us
    all_to_all x1, waiting for transfers between devices, on_device(): centers = lax.all_to_all(partial, PLANE, 0, 0, tiled=True)  8.35 us
    all_to_all x1, starting transfers between devices, on_device(): lax.all_to_all(rotated.reshape(128, 8, n), BAS, 0, 0, tiled=True)  6.89 us
  transfers between devices with their start and end apart: 6, of which 4 were waited for; matrix products, arithmetic and copies ran while one was open for 1% of the time, Pallas kernels for 4%

profile of v5, /device:TPU:1, one launch (start us, length us, event | category | flops | bytes accessed | tf_op | source)
XLA Modules:
  0.0 198.2 jit_solution(12553147107173757061)
XLA Ops:
  0.6 0.0 copy-start.4
  0.6 0.0 copy-start.5
  0.7 1.9 diagonal.1
  2.5 17.1 %all-to-all-start = ((f32[64,8,128]{2,1,0:T(8,128)}), f32[64,8,128]{2,1,0:T(8,128)S(1)}, u32[]{:S(2)}, u32[]{:S(2)}) async-start(f32[64,8,128]{2,1,0:T(8,128)} %diagonal.1), calls=%async_computation | async-start | bytes 524288 | tf_op jit(solution)/shard_map/all_to_all | solution.py:184
  19.6 2.9 %collective-permute-start = (bf16[3,128,256]{2,1,0:T(8,128)(2,1)}, bf16[3,128,256]{2,1,0:T(8,128)(2,1)S(1)}, u32[]{:S(2)}, u32[]{:S(2)}) collective-permute-start(bf16[3,128,256]{2,1,0:T(8,128)(2,1)} %d_own), channel_id=1, source_target_pairs={{0,4},{4,0},{1,5},{5,1},{2,6},{6,2},{3,7},{7,3},{8,12},{12,8},{9,1... | collective-permute-start | bytes 589832 | tf_op jit(solution)/shard_map/ppermute | solution.py:185
  22.6 1.2 copy.7
  23.8 0.0 collective-permute-done.d_other
  23.8 8.4 %all-to-all-done.parts = f32[64,8,128]{2,1,0:T(8,128)S(1)} async-done(((f32[64,8,128]{2,1,0:T(8,128)}), f32[64,8,128]{2,1,0:T(8,128)S(1)}, u32[]{:S(2)}, u32[]{:S(2)}) %all-to-all-start) | async-done | bytes 262176 | tf_op jit(solution)/shard_map/all_to_all | solution.py:184
  32.2 0.0 copy-done.5
  32.2 0.1 pack.1
  32.3 9.7 %all_to_all.30.met = bf16[4,2,160,128]{3,2,1,0:T(8,128)(2,1)S(1)} all-to-all(bf16[4,2,160,128]{3,2,1,0:T(8,128)(2,1)S(1)} %pack.1), channel_id=1, replica_groups=mesh['y'=8,'z'=8,'core'=2,'x'=4] {'x'}, dimensions={0} | all-to-all | bytes 655360 | tf_op jit(solution)/shard_map/all_to_all | solution.py:192
  42.0 0.0 copy-start.3
  42.0 6.7 %collective-permute-start.1 = (bf16[4,2,160,128]{3,2,1,0:T(8,128)(2,1)S(1)}, bf16[4,2,160,128]{3,2,1,0:T(8,128)(2,1)S(1)}, u32[]{:S(2)}, u32[]{:S(2)}) collective-permute-start(bf16[4,2,160,128]{3,2,1,0:T(8,128)(2,1)S(1)} %all_to_all.30.met), channel_id=1, source_target_pairs={{0,4},{4,0},{1,5},{5,1},{2,6},{6,2},{3,7},{7,3},{8,12},{12,8},{9,1... | collective-permute-start | bytes 983048 | tf_op jit(solution)/shard_map/ppermute | solution.py:193
  48.7 0.1 pad_add_fusion.place
  48.8 0.0 copy-start.6
  48.8 1.2 collective-permute-done.1.met_other
  50.0 0.0 copy-done.4
  50.0 1.3 gradient.1
  51.3 21.1 %all_to_all.31 = f32[64,16,128]{2,1,0:T(8,128)S(1)} all-to-all(f32[64,16,128]{2,1,0:T(8,128)S(1)} %gradient.1), channel_id=1, replica_groups=mesh['y'=8,'z'=8,'core'=2,'x'=4] {'y','z'}, dimensions={0} | all-to-all | bytes 1048576 | tf_op jit(solution)/shard_map/all_to_all | solution.py:201
  72.4 0.1 reduce_sum.9
  72.5 19.4 %all_to_all.32 = f16[64,16,128]{2,1,0:T(8,128)(2,1)S(1)} all-to-all(f16[64,16,128]{2,1,0:T(8,128)(2,1)S(1)} %broadcast_in_dim.4), channel_id=1, replica_groups=mesh['y'=8,'z'=8,'core'=2,'x'=4] {'y','z'}, dimensions={0} | all-to-all | bytes 524288 | tf_op jit(solution)/shard_map/all_to_all | solution.py:178
  92.0 0.1 broadcast_in_dim.5
  92.1 0.0 copy-done.3
  92.1 13.7 %all_to_all.33 = f16[4,64,16,128]{3,2,1,0:T(8,128)(2,1)S(1)} all-to-all(f16[4,64,16,128]{3,2,1,0:T(8,128)(2,1)S(1)} %broadcast_in_dim.5), channel_id=1, replica_groups=mesh['y'=8,'z'=8,'core'=2,'x'=4] {'x'}, dimensions={0} | all-to-all | bytes 2097152 | tf_op jit(solution)/shard_map/all_to_all | solution.py:178
  105.8 6.8 %collective-permute-start.2 = (f16[4,64,16,128]{3,2,1,0:T(8,128)(2,1)S(1)}, f16[4,64,16,128]{3,2,1,0:T(8,128)(2,1)S(1)}, u32[]{:S(2)}, u32[]{:S(2)}) collective-permute-start(f16[4,64,16,128]{3,2,1,0:T(8,128)(2,1)S(1)} %all_to_all.33), channel_id=1, source_target_pairs={{0,4},{4,0},{1,5},{5,1},{2,6},{6,2},{3,7},{7,3},{8,12},{12,8},{9,1... | collective-permute-start | bytes 3145736 | tf_op jit(solution)/shard_map/ppermute | solution.py:204
  112.7 0.4 fusion
  113.1 2.5 %square.1.near_square = f32[1024,512]{1,0:T(8,128)S(1)} custom-call(s32[2]{0:T(128)S(1)} %pad_add_fusion.place, bf16[4,64,16,128]{3,2,1,0:T(8,128)(2,1)S(1)} %get-tuple-element.21.own_h, bf16[4,64,16,128]{3,2,1,0:T(8,128)(2,1)S(1)} %get-tuple-element.20.own_l), custom_call_target="tpu_custom_call" | custom-call | flops 1610612736 | bytes 4194304 | tf_op jit(solution)/shard_map/square/pallas_call | solution.py:213
  115.6 0.0 collective-permute-done.2
  115.6 0.4 fusion.1
  116.0 0.0 copy-start.1
  116.1 14.0 %series.1.rot_own = bf16[1024,512]{1,0:T(8,128)(2,1)S(1)} custom-call(s32[2]{0:T(128)S(1)} %pad_add_fusion.place, f32[1024,512]{1,0:T(8,128)S(1)} %square.1.near_square, bf16[4,64,16,128]{3,2,1,0:T(8,128)(2,1)S(1)} %get-tuple-element.21.own_h, bf16[4,64,16,128]{3,2,1,0:T(8,128)(2,1)S(1)} %get-tuple-element.20.own_l, ...), custom_call_target="tpu_custom_call" | custom-call | tf_op jit(solution)/shard_map/series/pallas_call | solution.py:222
  130.0 0.0 copy-start
  130.0 1.9 collective-permute-start.3
  132.0 0.0 copy-done.1
  132.0 2.0 near.1.near_part
  133.9 0.0 copy-done
  133.9 0.6 collective-permute-done.3.rot_other
  134.6 0.0 copy-done.6
  134.6 0.0 copy-start.2
  134.6 3.3 %rotate.1 = bf16[1024,1024]{1,0:T(8,128)(2,1)} custom-call(s32[2]{0:T(128)S(1)} %pad_add_fusion.place, f32[1024,1024]{1,0:T(8,128)S(1)} %near.1.near_part, bf16[1024,512]{1,0:T(8,128)(2,1)S(1)} %collective-permute-done.3.rot_other, bf16[1024,1024]{1,0:T(8,128)(2,1)S(1)} %bitcast.7), custom_call_target="tpu_custom_call" | custom-call | tf_op jit(solution)/shard_map/rotate/pallas_call | solution.py:239
  137.9 0.0 copy-done.2
  137.9 6.9 %all-to-all-start.5 = ((bf16[128,8,1024]{2,1,0:T(8,128)(2,1)}), bf16[128,8,1024]{2,1,0:T(8,128)(2,1)S(1)}, u32[]{:S(2)}, u32[]{:S(2)}) async-start(bf16[128,8,1024]{2,1,0:T(8,128)(2,1)} %bitcast.4), calls=%async_computation.5 | async-start | bytes 4194304 | tf_op jit(solution)/shard_map/all_to_all | solution.py:246
  144.8 2.6 %new_orbitals.1 = bf16[128,256]{1,0:T(8,128)(2,1)} custom-call(s32[2]{0:T(128)} %copy-done.6, bf16[1024,512]{1,0:T(8,128)(2,1)} %copy-done, bf16[1024,512]{1,0:T(8,128)(2,1)} %copy-done.2, bf16[4,2,160,128]{3,2,1,0:T(8,128)(2,1)} %copy-done.3), custom_call_target="tpu_custom_call" | custom-call | tf_op jit(solution)/shard_map/new_orbitals/pallas_call | solution.py:247
  147.3 49.6 %all-to-all-done.5 = bf16[128,8,1024]{2,1,0:T(8,128)(2,1)S(1)} async-done(((bf16[128,8,1024]{2,1,0:T(8,128)(2,1)}), bf16[128,8,1024]{2,1,0:T(8,128)(2,1)S(1)}, u32[]{:S(2)}, u32[]{:S(2)}) %all-to-all-start.5) | async-done | bytes 2097184 | tf_op jit(solution)/shard_map/all_to_all | solution.py:246
  196.9 1.3 copy.9
  (3 shorter events, 0.1 us)
Async XLA Ops:
  0.6 49.3 %copy-start.4 = (bf16[3,128,256]{2,1,0:T(8,128)(2,1)S(1)}, bf16[3,128,256]{2,1,0:T(8,128)(2,1)}, u32[]{:S(2)}) copy-start(bf16[3,128,256]{2,1,0:T(8,128)(2,1)} %d_own) | copy-start | bytes 589828
  0.6 31.6 %copy-start.5 = (bf16[128,256]{1,0:T(8,128)(2,1)S(1)}, bf16[128,256]{1,0:T(8,128)(2,1)}, u32[]{:S(2)}) copy-start(bf16[128,256]{1,0:T(8,128)(2,1)} %orb.3) | copy-start | bytes 196612
  2.5 29.7 %all-to-all-start = ((f32[64,8,128]{2,1,0:T(8,128)}), f32[64,8,128]{2,1,0:T(8,128)S(1)}, u32[]{:S(2)}, u32[]{:S(2)}) async-start(f32[64,8,128]{2,1,0:T(8,128)} %diagonal.1), calls=%async_computation | async-start | bytes 524288 | tf_op jit(solution)/shard_map/all_to_all | solution.py:184
  19.6 4.2 %collective-permute-start = (bf16[3,128,256]{2,1,0:T(8,128)(2,1)}, bf16[3,128,256]{2,1,0:T(8,128)(2,1)S(1)}, u32[]{:S(2)}, u32[]{:S(2)}) collective-permute-start(bf16[3,128,256]{2,1,0:T(8,128)(2,1)} %d_own), channel_id=1, source_target_pairs={{0,4},{4,0},{1,5},{5,1},{2,6},{6,2},{3,7},{7,3},{8,12},{12,8},{9,1... | collective-permute-start | bytes 589832 | tf_op jit(solution)/shard_map/ppermute | solution.py:185
  42.0 50.1 %copy-start.3 = (bf16[4,2,160,128]{3,2,1,0:T(8,128)(2,1)}, bf16[4,2,160,128]{3,2,1,0:T(8,128)(2,1)S(1)}, u32[]{:S(2)}) copy-start(bf16[4,2,160,128]{3,2,1,0:T(8,128)(2,1)S(1)} %all_to_all.30.met) | copy-start | bytes 983044
  42.0 8.0 %collective-permute-start.1 = (bf16[4,2,160,128]{3,2,1,0:T(8,128)(2,1)S(1)}, bf16[4,2,160,128]{3,2,1,0:T(8,128)(2,1)S(1)}, u32[]{:S(2)}, u32[]{:S(2)}) collective-permute-start(bf16[4,2,160,128]{3,2,1,0:T(8,128)(2,1)S(1)} %all_to_all.30.met), channel_id=1, source_target_pairs={{0,4},{4,0},{1,5},{5,1},{2,6},{6,2},{3,7},{7,3},{8,12},{12,8},{9,1... | collective-permute-start | bytes 983048 | tf_op jit(solution)/shard_map/ppermute | solution.py:193
  48.8 85.8 %copy-start.6 = (s32[2]{0:T(128)}, s32[2]{0:T(128)S(1)}, u32[]{:S(2)}) copy-start(s32[2]{0:T(128)S(1)} %pad_add_fusion.place) | copy-start | bytes 28
  105.8 9.8 %collective-permute-start.2 = (f16[4,64,16,128]{3,2,1,0:T(8,128)(2,1)S(1)}, f16[4,64,16,128]{3,2,1,0:T(8,128)(2,1)S(1)}, u32[]{:S(2)}, u32[]{:S(2)}) collective-permute-start(f16[4,64,16,128]{3,2,1,0:T(8,128)(2,1)S(1)} %all_to_all.33), channel_id=1, source_target_pairs={{0,4},{4,0},{1,5},{5,1},{2,6},{6,2},{3,7},{7,3},{8,12},{12,8},{9,1... | collective-permute-start | bytes 3145736 | tf_op jit(solution)/shard_map/ppermute | solution.py:204
  116.0 15.9 %copy-start.1 = (bf16[1,1024,1024]{2,1,0:T(8,128)(2,1)S(1)}, bf16[1,1024,1024]{2,1,0:T(8,128)(2,1)}, u32[]{:S(2)}) copy-start(bf16[1,1024,1024]{2,1,0:T(8,128)(2,1)} %param.7) | copy-start | bytes 6291460
  130.0 3.9 %copy-start = (bf16[1024,512]{1,0:T(8,128)(2,1)}, bf16[1024,512]{1,0:T(8,128)(2,1)S(1)}, u32[]{:S(2)}) copy-start(bf16[1024,512]{1,0:T(8,128)(2,1)S(1)} %series.1.rot_own) | copy-start | bytes 3145732
  130.0 4.6 %collective-permute-start.3 = (bf16[1024,512]{1,0:T(8,128)(2,1)S(1)}, bf16[1024,512]{1,0:T(8,128)(2,1)S(1)}, u32[]{:S(2)}, u32[]{:S(2)}) collective-permute-start(bf16[1024,512]{1,0:T(8,128)(2,1)S(1)} %series.1.rot_own), channel_id=1, source_target_pairs={{0,4},{4,0},{1,5},{5,1},{2,6},{6,2},{3,7},{7,3},{8,12},{12,8},{9,1... | collective-permute-start | bytes 3145736 | tf_op jit(solution)/shard_map/ppermute | solution.py:230
  134.6 3.3 %copy-start.2 = (bf16[1024,512]{1,0:T(8,128)(2,1)}, bf16[1024,512]{1,0:T(8,128)(2,1)S(1)}, u32[]{:S(2)}) copy-start(bf16[1024,512]{1,0:T(8,128)(2,1)S(1)} %collective-permute-done.3.rot_other) | copy-start | bytes 3145732
  137.9 59.0 %all-to-all-start.5 = ((bf16[128,8,1024]{2,1,0:T(8,128)(2,1)}), bf16[128,8,1024]{2,1,0:T(8,128)(2,1)S(1)}, u32[]{:S(2)}, u32[]{:S(2)}) async-start(bf16[128,8,1024]{2,1,0:T(8,128)(2,1)} %bitcast.4), calls=%async_computation.5 | async-start | bytes 4194304 | tf_op jit(solution)/shard_map/all_to_all | solution.py:246

commit v6 on v5

--- a/solution.py
+++ b/solution.py
@@ -39,23 +39,36 @@
     rest = total - first.astype(F32)
     second = rest.astype(BF16)
     third = (rest - second.astype(F32)).astype(BF16)
-    tail = jnp.concatenate([first, second, third, jnp.zeros((8, 128), BF16)], axis=0)
+    tails = (
+        jnp.concatenate([first, second], axis=0),
+        jnp.concatenate([third, jnp.zeros((8, 128), BF16)], axis=0),
+    )
     for d in range(out.shape[0]):
         out[d, 0, :128] = orb[:, :128]
         out[d, 1, :128] = orb[:, 128:]
-        out[d, 0, 128:] = tail
-        out[d, 1, 128:] = jnp.zeros((32, 128), BF16)
-
-
-def gradient_kernel(scale, place, met, met_other, d_own, d_other, out):
+        out[d, 0, 128:] = tails[0]
+        out[d, 1, 128:] = tails[1]
+
+
+CONTRACT = (((0,), (0,)), ((), ()))
+
+
+def moment_kernel(place, met, d_own, out):
+    for half in range(2):
+        for g in range(2):
+            for k in range(3):
+                rows = met[2 * place[0] + half, g, :128]
+                out[k, 2 * half + g] = lax.dot_general(d_own[k], rows, CONTRACT, preferred_element_type=F32)
+
+
+def gradient_kernel(scale, place, met, met_other, near, d_other, out):
     core, orb = place[0], place[1]
-    contract = (((0,), (0,)), ((), ()))
 
     def centers(block):
         total = jnp.zeros((8, 128), F32)
         for source in (met, met_other):
-            tail = source[block, 0, 128:].astype(F32)
-            total = total + (tail[0:8] + tail[8:16] + tail[16:24])
+            large, small = source[block, 0, 128:].astype(F32), source[block, 1, 128:].astype(F32)
+            total = total + (large[0:8] + large[8:16] + small[0:8])
         return total
 
     mine = centers(orb)
@@ -67,9 +80,8 @@
         for g in range(2):
             total = None
             for k in range(3):
-                moment = lax.dot_general(d_own[k], met[block, g, :128], contract, preferred_element_type=F32)
-                moment += lax.dot_general(
-                    d_other[k], met_other[block, g, :128], contract, preferred_element_type=F32
+                moment = near[k, 2 * half + g] + lax.dot_general(
+                    d_other[k], met_other[block, g, :128], CONTRACT, preferred_element_type=F32
                 )
                 term = moment * (cen_i[2 * k + g : 2 * k + g + 1] - cen_j[k])
                 total = term if total is None else total + term
@@ -186,18 +198,26 @@
     centers, d_other = lax.optimization_barrier((centers, d_other))
     given = lax.dynamic_slice(given, (core * 512 + (spot % 4) * 128, (spot // 4) * 16), (128, 16)).astype(F32).T
     packed = pl.pallas_call(
-        pack_kernel, out_shape=jax.ShapeDtypeStruct((4, 2, nbas + 32, 128), BF16), compiler_params=grant(6), name="pack"
+        pack_kernel, out_shape=jax.ShapeDtypeStruct((4, 2, nbas + 16, 128), BF16), compiler_params=grant(6), name="pack"
     )(centers, orbitals)
     packed, d_here, given = lax.optimization_barrier((packed, d_here, given))
     met = lax.all_to_all(packed, "x", 0, 0, tiled=True)
     met_other = lax.ppermute(met, "core", swap)
+    near = pl.pallas_call(
+        moment_kernel,
+        out_shape=jax.ShapeDtypeStruct((3, 4, block, 128), F32),
+        in_specs=[SMEM] + [VMEM] * 2,
+        compiler_params=grant(8),
+        cost_estimate=pl.CostEstimate(flops=1 << 28, bytes_accessed=2 << 20, transcendentals=0),
+        name="moments",
+    )(place, met, d_here)
     pieces = pl.pallas_call(
         functools.partial(gradient_kernel, scale),
         out_shape=jax.ShapeDtypeStruct((64, 16, 128), F32),
         in_specs=[SMEM] + [VMEM] * 4,
         compiler_params=grant(8),
         name="gradient",
-    )(place, met, met_other, d_here, d_other)
+    )(place, met, met_other, near, d_other)
     piece = jnp.sum(lax.all_to_all(pieces, PLANE, 0, 0, tiled=True), axis=0) + given
     wire = (piece * WIRE_SCALE).astype(F16)
     half = spread(spread(wire, PLANE, 64), "x", 4)

time: 199 us -> 199 us (level)
  no operation moved by 1% of the time
where the time goes in v6:
time: 199 us; the launch traced here: 198 us
  blocking collectives  63.8 us (32%)
  waiting for transfers between devices  58.8 us (30%)
  starting transfers between devices  42.3 us (21%)
  Pallas kernels  28.4 us (14%)
  local copies, waits for them, and re-layouts  2.78 us (1%)
    all_to_all x1, waiting for transfers between devices, on_device(): lax.all_to_all(rotated.reshape(128, 8, n), BAS, 0, 0, tiled=True)  49.6 us
    all_to_all x2, blocking collectives, spread(): return lax.all_to_all(copies, axes, 0, 0, tiled=True)  33.2 us
    all_to_all x1, blocking collectives, on_device(): lax.all_to_all(pieces, PLANE, 0, 0, tiled=True)  21.1 us
    all_to_all x1, starting transfers between devices, on_device(): centers = lax.all_to_all(partial, PLANE, 0, 0, tiled=True)  17.1 us
    pallas_call x1, Pallas kernels, on_device(): pl.pallas_call(series_kernel, out_shape=jax.ShapeDtypeStruct((n, n // 2),...  14 us
    all_to_all x1, blocking collectives, on_device(): met = lax.all_to_all(packed, 'x', 0, 0, tiled=True)  9.52 us
    all_to_all x1, waiting for transfers between devices, on_device(): centers = lax.all_to_all(partial, PLANE, 0, 0, tiled=True)  8.35 us
    all_to_all x1, starting transfers between devices, on_device(): lax.all_to_all(rotated.reshape(128, 8, n), BAS, 0, 0, tiled=True)  6.87 us
  transfers between devices with their start and end apart: 6, of which 4 were waited for; matrix products, arithmetic and copies ran while one was open for 1% of the time, Pallas kernels for 4%

profile of v6, /device:TPU:1, one launch (start us, length us, event | category | flops | bytes accessed | tf_op | source)
XLA Modules:
  0.0 197.9 jit_solution(10338090992297087781)
XLA Ops:
  0.6 0.0 copy-start.4
  0.6 0.0 copy-start.5
  0.7 1.9 diagonal.1
  2.5 17.1 %all-to-all-start = ((f32[64,8,128]{2,1,0:T(8,128)}), f32[64,8,128]{2,1,0:T(8,128)S(1)}, u32[]{:S(2)}, u32[]{:S(2)}) async-start(f32[64,8,128]{2,1,0:T(8,128)} %diagonal.1), calls=%async_computation | async-start | bytes 524288 | tf_op jit(solution)/shard_map/all_to_all | solution.py:196
  19.6 2.9 %collective-permute-start = (bf16[3,128,256]{2,1,0:T(8,128)(2,1)}, bf16[3,128,256]{2,1,0:T(8,128)(2,1)S(1)}, u32[]{:S(2)}, u32[]{:S(2)}) collective-permute-start(bf16[3,128,256]{2,1,0:T(8,128)(2,1)} %d_own), channel_id=1, source_target_pairs={{0,4},{4,0},{1,5},{5,1},{2,6},{6,2},{3,7},{7,3},{8,12},{12,8},{9,1... | collective-permute-start | bytes 589832 | tf_op jit(solution)/shard_map/ppermute | solution.py:197
  22.6 1.2 copy.7
  23.8 0.0 collective-permute-done.d_other
  23.8 8.4 %all-to-all-done.parts = f32[64,8,128]{2,1,0:T(8,128)S(1)} async-done(((f32[64,8,128]{2,1,0:T(8,128)}), f32[64,8,128]{2,1,0:T(8,128)S(1)}, u32[]{:S(2)}, u32[]{:S(2)}) %all-to-all-start) | async-done | bytes 262176 | tf_op jit(solution)/shard_map/all_to_all | solution.py:196
  32.2 0.0 copy-done.5
  32.2 0.1 pack.1
  32.3 9.5 %all_to_all.30.met = bf16[4,2,144,128]{3,2,1,0:T(8,128)(2,1)S(1)} all-to-all(bf16[4,2,144,128]{3,2,1,0:T(8,128)(2,1)S(1)} %pack.1), channel_id=1, replica_groups=mesh['y'=8,'z'=8,'core'=2,'x'=4] {'x'}, dimensions={0} | all-to-all | bytes 589824 | tf_op jit(solution)/shard_map/all_to_all | solution.py:204
  41.8 0.0 copy-start.2
  41.8 6.7 %collective-permute-start.1 = (bf16[4,2,144,128]{3,2,1,0:T(8,128)(2,1)S(1)}, bf16[4,2,144,128]{3,2,1,0:T(8,128)(2,1)S(1)}, u32[]{:S(2)}, u32[]{:S(2)}) collective-permute-start(bf16[4,2,144,128]{3,2,1,0:T(8,128)(2,1)S(1)} %all_to_all.30.met), channel_id=1, source_target_pairs={{0,4},{4,0},{1,5},{5,1},{2,6},{6,2},{3,7},{7,3},{8,12},{12,8},{9,1... | collective-permute-start | bytes 884744 | tf_op jit(solution)/shard_map/ppermute | solution.py:205
  48.5 0.1 pad_add_fusion.place
  48.6 0.0 copy-done.4
  48.6 0.0 copy-start.6
  48.6 0.9 moments.1.near
  49.6 0.2 collective-permute-done.1.met_other
  49.7 1.2 gradient.1
  50.9 0.0 copy-done.2
  50.9 21.1 %all_to_all.31 = f32[64,16,128]{2,1,0:T(8,128)S(1)} all-to-all(f32[64,16,128]{2,1,0:T(8,128)S(1)} %gradient.1), channel_id=1, replica_groups=mesh['y'=8,'z'=8,'core'=2,'x'=4] {'y','z'}, dimensions={0} | all-to-all | bytes 1048576 | tf_op jit(solution)/shard_map/all_to_all | solution.py:221
  72.0 0.1 reduce_sum.9
  72.2 19.4 %all_to_all.32 = f16[64,16,128]{2,1,0:T(8,128)(2,1)S(1)} all-to-all(f16[64,16,128]{2,1,0:T(8,128)(2,1)S(1)} %broadcast_in_dim.4), channel_id=1, replica_groups=mesh['y'=8,'z'=8,'core'=2,'x'=4] {'y','z'}, dimensions={0} | all-to-all | bytes 524288 | tf_op jit(solution)/shard_map/all_to_all | solution.py:190
  91.6 0.1 broadcast_in_dim.5
  91.8 13.7 %all_to_all.33 = f16[4,64,16,128]{3,2,1,0:T(8,128)(2,1)S(1)} all-to-all(f16[4,64,16,128]{3,2,1,0:T(8,128)(2,1)S(1)} %broadcast_in_dim.5), channel_id=1, replica_groups=mesh['y'=8,'z'=8,'core'=2,'x'=4] {'x'}, dimensions={0} | all-to-all | bytes 2097152 | tf_op jit(solution)/shard_map/all_to_all | solution.py:190
  105.5 6.8 %collective-permute-start.2 = (f16[4,64,16,128]{3,2,1,0:T(8,128)(2,1)S(1)}, f16[4,64,16,128]{3,2,1,0:T(8,128)(2,1)S(1)}, u32[]{:S(2)}, u32[]{:S(2)}) collective-permute-start(f16[4,64,16,128]{3,2,1,0:T(8,128)(2,1)S(1)} %all_to_all.33), channel_id=1, source_target_pairs={{0,4},{4,0},{1,5},{5,1},{2,6},{6,2},{3,7},{7,3},{8,12},{12,8},{9,1... | collective-permute-start | bytes 3145736 | tf_op jit(solution)/shard_map/ppermute | solution.py:224
  112.3 0.4 fusion
  112.7 2.5 %square.1.near_square = f32[1024,512]{1,0:T(8,128)S(1)} custom-call(s32[2]{0:T(128)S(1)} %pad_add_fusion.place, bf16[4,64,16,128]{3,2,1,0:T(8,128)(2,1)S(1)} %get-tuple-element.21.own_h, bf16[4,64,16,128]{3,2,1,0:T(8,128)(2,1)S(1)} %get-tuple-element.20.own_l), custom_call_target="tpu_custom_call" | custom-call | flops 1610612736 | bytes 4194304 | tf_op jit(solution)/shard_map/square/pallas_call | solution.py:233
  115.3 0.0 collective-permute-done.2
  115.3 0.4 fusion.1
  115.7 0.0 copy-start.1
  115.7 14.0 %series.1.rot_own = bf16[1024,512]{1,0:T(8,128)(2,1)S(1)} custom-call(s32[2]{0:T(128)S(1)} %pad_add_fusion.place, f32[1024,512]{1,0:T(8,128)S(1)} %square.1.near_square, bf16[4,64,16,128]{3,2,1,0:T(8,128)(2,1)S(1)} %get-tuple-element.21.own_h, bf16[4,64,16,128]{3,2,1,0:T(8,128)(2,1)S(1)} %get-tuple-element.20.own_l, ...), custom_call_target="tpu_custom_call" | custom-call | tf_op jit(solution)/shard_map/series/pallas_call | solution.py:242
  129.7 0.0 copy-start
  129.7 1.9 collective-permute-start.3
  131.6 0.0 copy-done.1
  131.6 2.0 near.1.near_part
  133.6 0.0 copy-done
  133.6 0.6 collective-permute-done.3.rot_other
  134.2 0.0 copy-done.6
  134.2 0.0 copy-start.3
  134.2 3.3 %rotate.1 = bf16[1024,1024]{1,0:T(8,128)(2,1)} custom-call(s32[2]{0:T(128)S(1)} %pad_add_fusion.place, f32[1024,1024]{1,0:T(8,128)S(1)} %near.1.near_part, bf16[1024,512]{1,0:T(8,128)(2,1)S(1)} %collective-permute-done.3.rot_other, bf16[1024,1024]{1,0:T(8,128)(2,1)S(1)} %bitcast.7), custom_call_target="tpu_custom_call" | custom-call | tf_op jit(solution)/shard_map/rotate/pallas_call | solution.py:259
  137.5 0.0 copy-done.3
  137.5 6.9 %all-to-all-start.5 = ((bf16[128,8,1024]{2,1,0:T(8,128)(2,1)}), bf16[128,8,1024]{2,1,0:T(8,128)(2,1)S(1)}, u32[]{:S(2)}, u32[]{:S(2)}) async-start(bf16[128,8,1024]{2,1,0:T(8,128)(2,1)} %bitcast.4), calls=%async_computation.5 | async-start | bytes 4194304 | tf_op jit(solution)/shard_map/all_to_all | solution.py:266
  144.4 2.5 %new_orbitals.1 = bf16[128,256]{1,0:T(8,128)(2,1)} custom-call(s32[2]{0:T(128)} %copy-done.6, bf16[1024,512]{1,0:T(8,128)(2,1)} %copy-done, bf16[1024,512]{1,0:T(8,128)(2,1)} %copy-done.3, bf16[4,2,144,128]{3,2,1,0:T(8,128)(2,1)} %copy-done.2), custom_call_target="tpu_custom_call" | custom-call | tf_op jit(solution)/shard_map/new_orbitals/pallas_call | solution.py:267
  147.0 49.6 %all-to-all-done.5 = bf16[128,8,1024]{2,1,0:T(8,128)(2,1)S(1)} async-done(((bf16[128,8,1024]{2,1,0:T(8,128)(2,1)}), bf16[128,8,1024]{2,1,0:T(8,128)(2,1)S(1)}, u32[]{:S(2)}, u32[]{:S(2)}) %all-to-all-start.5) | async-done | bytes 2097184 | tf_op jit(solution)/shard_map/all_to_all | solution.py:266
  196.6 1.3 copy.9
  (3 shorter events, 0.1 us)
Async XLA Ops:
  0.6 48.0 %copy-start.4 = (bf16[3,128,256]{2,1,0:T(8,128)(2,1)S(1)}, bf16[3,128,256]{2,1,0:T(8,128)(2,1)}, u32[]{:S(2)}) copy-start(bf16[3,128,256]{2,1,0:T(8,128)(2,1)} %d_own) | copy-start | bytes 589828
  0.6 31.6 %copy-start.5 = (bf16[128,256]{1,0:T(8,128)(2,1)S(1)}, bf16[128,256]{1,0:T(8,128)(2,1)}, u32[]{:S(2)}) copy-start(bf16[128,256]{1,0:T(8,128)(2,1)} %orb.3) | copy-start | bytes 196612
  2.5 29.7 %all-to-all-start = ((f32[64,8,128]{2,1,0:T(8,128)}), f32[64,8,128]{2,1,0:T(8,128)S(1)}, u32[]{:S(2)}, u32[]{:S(2)}) async-start(f32[64,8,128]{2,1,0:T(8,128)} %diagonal.1), calls=%async_computation | async-start | bytes 524288 | tf_op jit(solution)/shard_map/all_to_all | solution.py:196
  19.6 4.2 %collective-permute-start = (bf16[3,128,256]{2,1,0:T(8,128)(2,1)}, bf16[3,128,256]{2,1,0:T(8,128)(2,1)S(1)}, u32[]{:S(2)}, u32[]{:S(2)}) collective-permute-start(bf16[3,128,256]{2,1,0:T(8,128)(2,1)} %d_own), channel_id=1, source_target_pairs={{0,4},{4,0},{1,5},{5,1},{2,6},{6,2},{3,7},{7,3},{8,12},{12,8},{9,1... | collective-permute-start | bytes 589832 | tf_op jit(solution)/shard_map/ppermute | solution.py:197
  41.8 9.1 %copy-start.2 = (bf16[4,2,144,128]{3,2,1,0:T(8,128)(2,1)}, bf16[4,2,144,128]{3,2,1,0:T(8,128)(2,1)S(1)}, u32[]{:S(2)}) copy-start(bf16[4,2,144,128]{3,2,1,0:T(8,128)(2,1)S(1)} %all_to_all.30.met) | copy-start | bytes 884740
  41.8 7.9 %collective-permute-start.1 = (bf16[4,2,144,128]{3,2,1,0:T(8,128)(2,1)S(1)}, bf16[4,2,144,128]{3,2,1,0:T(8,128)(2,1)S(1)}, u32[]{:S(2)}, u32[]{:S(2)}) collective-permute-start(bf16[4,2,144,128]{3,2,1,0:T(8,128)(2,1)S(1)} %all_to_all.30.met), channel_id=1, source_target_pairs={{0,4},{4,0},{1,5},{5,1},{2,6},{6,2},{3,7},{7,3},{8,12},{12,8},{9,1... | collective-permute-start | bytes 884744 | tf_op jit(solution)/shard_map/ppermute | solution.py:205
  48.6 85.6 %copy-start.6 = (s32[2]{0:T(128)}, s32[2]{0:T(128)S(1)}, u32[]{:S(2)}) copy-start(s32[2]{0:T(128)S(1)} %pad_add_fusion.place) | copy-start | bytes 28
  105.5 9.8 %collective-permute-start.2 = (f16[4,64,16,128]{3,2,1,0:T(8,128)(2,1)S(1)}, f16[4,64,16,128]{3,2,1,0:T(8,128)(2,1)S(1)}, u32[]{:S(2)}, u32[]{:S(2)}) collective-permute-start(f16[4,64,16,128]{3,2,1,0:T(8,128)(2,1)S(1)} %all_to_all.33), channel_id=1, source_target_pairs={{0,4},{4,0},{1,5},{5,1},{2,6},{6,2},{3,7},{7,3},{8,12},{12,8},{9,1... | collective-permute-start | bytes 3145736 | tf_op jit(solution)/shard_map/ppermute | solution.py:224
  115.7 15.9 %copy-start.1 = (bf16[1,1024,1024]{2,1,0:T(8,128)(2,1)S(1)}, bf16[1,1024,1024]{2,1,0:T(8,128)(2,1)}, u32[]{:S(2)}) copy-start(bf16[1,1024,1024]{2,1,0:T(8,128)(2,1)} %param.7) | copy-start | bytes 6291460
  129.7 3.9 %copy-start = (bf16[1024,512]{1,0:T(8,128)(2,1)}, bf16[1024,512]{1,0:T(8,128)(2,1)S(1)}, u32[]{:S(2)}) copy-start(bf16[1024,512]{1,0:T(8,128)(2,1)S(1)} %series.1.rot_own) | copy-start | bytes 3145732
  129.7 4.6 %collective-permute-start.3 = (bf16[1024,512]{1,0:T(8,128)(2,1)S(1)}, bf16[1024,512]{1,0:T(8,128)(2,1)S(1)}, u32[]{:S(2)}, u32[]{:S(2)}) collective-permute-start(bf16[1024,512]{1,0:T(8,128)(2,1)S(1)} %series.1.rot_own), channel_id=1, source_target_pairs={{0,4},{4,0},{1,5},{5,1},{2,6},{6,2},{3,7},{7,3},{8,12},{12,8},{9,1... | collective-permute-start | bytes 3145736 | tf_op jit(solution)/shard_map/ppermute | solution.py:250
  134.2 3.3 %copy-start.3 = (bf16[1024,512]{1,0:T(8,128)(2,1)}, bf16[1024,512]{1,0:T(8,128)(2,1)S(1)}, u32[]{:S(2)}) copy-start(bf16[1024,512]{1,0:T(8,128)(2,1)S(1)} %collective-permute-done.3.rot_other) | copy-start | bytes 3145732
  137.5 59.0 %all-to-all-start.5 = ((bf16[128,8,1024]{2,1,0:T(8,128)(2,1)}), bf16[128,8,1024]{2,1,0:T(8,128)(2,1)S(1)}, u32[]{:S(2)}, u32[]{:S(2)}) async-start(bf16[128,8,1024]{2,1,0:T(8,128)(2,1)} %bitcast.4), calls=%async_computation.5 | async-start | bytes 4194304 | tf_op jit(solution)/shard_map/all_to_all | solution.py:266
